TPU v7x, 32 devices: a whole 2x2x4 slice. The times are simulated.
32 devices in a mesh: gx: 16 (over z, y, x), gy: 2 (over core).
Axes of the slice: x: 2, y: 2, z: 4, core: 2. Of those that a mesh axis runs over, the one named last changes fastest.
Arguments:
- adjoint_init: float32 [3, 128, 16, 256], P(None, 'gx', 'gy'), may hold values from -6 to 6
- saved_states: bfloat16 [4, 3, 128, 16, 256], P(None, None, 'gx', 'gy'), may hold values from -4 to 4
- step_index: int32 [4], replicated, may hold values from 0 to 3
- vertical_inverse: float32 [256, 256], replicated, may hold values from -1 to 2
- disk_filter: bfloat16 [16, 2, 8, 64, 512], P('gx', 'gy'), may hold values from -0.25 to 0.25
- pair_turbine: int32 [16, 2, 8], P('gx', 'gy'), may hold values from 0 to 24, as said below
- pair_tile: int32 [16, 2, 8], P('gx', 'gy'), may hold values from 0 to 31
- turbine_owner: int32 [24], replicated, may hold values from 0 to 31
Outputs:
- adjoint_final: float32 [3, 128, 16, 256], P(None, 'gx', 'gy')
- turbine_grad: float32 [16, 2, 24], P('gx', 'gy')
Inputs may be any that keep to these rules, and one draw needn't show every extreme that they name: `pair_turbine`: entry 24 marks an empty slot.
All inputs are finite; a program needn't handle non-finite values.
Results may differ from a plain program's by a relative error of at most 0.0024.
Values may be sent and summed in bfloat16 or wider, within the bound.
A program may use at most 64 MiB of HBM per device.

v0:
```python
import jax
import jax.numpy as jnp
from jax import lax
from jax.sharding import PartitionSpec as P

STEPS = 4


COURANT = 0.2


def extended(block, sides, width):
    for axis, dim in sides:
        count = lax.axis_size(axis)
        forward = [(i, i + 1) for i in range(count - 1)]
        forward.append((count - 1, 0))
        backward = [(target, source) for source, target in forward]
        low = lax.ppermute(
            lax.slice_in_dim(block, block.shape[dim] - width, None, axis=dim), axis, forward
        )
        high = lax.ppermute(lax.slice_in_dim(block, 0, width, axis=dim), axis, backward)
        block = jnp.concatenate([low, block, high], axis=dim)
    return block


def vertical_difference(values):
    padded = jnp.pad(values, ((0, 0), (0, 0), (0, 0), (1, 1)))
    return 0.5 * (padded[..., 2:] - padded[..., :-2])


def planar_differences(stream_rim, span_rim):
    return (
        0.5 * (stream_rim[:, 2:] - stream_rim[:, :-2]),
        0.5 * (span_rim[:, :, 2:] - span_rim[:, :, :-2]),
    )


def adjoint_rims(values):
    padded = extended(values, (("gx", 1), ("gy", 2)), 1)
    return (padded[:, :, 1:-1], padded[:, 1:-1, :])


def states_rims(values):
    padded = extended(values, (("gx", 2), ("gy", 3)), 1)
    return (padded[:, :, :, 1:-1], padded[:, :, 1:-1, :])


def body(
    adjoint_init,
    saved_states,
    step_index,
    vertical_inverse,
    disk_filter,
    pair_turbine,
    pair_tile,
    turbine_owner,
):
    stream_cols = adjoint_init.shape[1]
    span_cols = adjoint_init.shape[2]
    levels = adjoint_init.shape[3]
    turbines = turbine_owner.shape[0]
    tile_rows = stream_cols * span_cols // 2
    filters = disk_filter[0, 0]
    slot_tiles = pair_tile[0, 0]
    matches = (
        pair_turbine[0, 0][:, None] == jnp.arange(turbines, dtype=jnp.int32)[None, :]
    ).astype(jnp.float32)
    adjoint = adjoint_init
    totals = jnp.zeros((turbines,), jnp.float32)
    all_stream_rims, all_span_rims = states_rims(saved_states)
    for number in range(STEPS):
        stored = lax.dynamic_index_in_dim(saved_states, step_index[number], 0, keepdims=False)
        forward_stream_rim = lax.dynamic_index_in_dim(
            all_stream_rims, step_index[number], 0, keepdims=False
        )
        forward_span_rim = lax.dynamic_index_in_dim(
            all_span_rims, step_index[number], 0, keepdims=False
        )
        forward_stream, forward_span = planar_differences(
            forward_stream_rim.astype(jnp.float32), forward_span_rim.astype(jnp.float32)
        )
        velocity = stored.astype(jnp.float32)
        forward_depth = vertical_difference(velocity)
        solved = jnp.dot(
            adjoint.reshape(-1, levels),
            vertical_inverse,
            precision=lax.Precision.HIGHEST,
            preferred_element_type=jnp.float32,
        ).reshape(adjoint.shape)
        solved_stream_rim, solved_span_rim = adjoint_rims(solved)
        solved_stream, solved_span = planar_differences(solved_stream_rim, solved_span_rim)
        solved_depth = vertical_difference(solved)
        advect = (
            velocity[0:1] * solved_stream
            + velocity[1:2] * solved_span
            + velocity[2:3] * solved_depth
        )
        derivs = (forward_stream, forward_span, forward_depth)
        couple = jnp.stack(
            [
                solved[0] * derivs[component][0]
                + solved[1] * derivs[component][1]
                + solved[2] * derivs[component][2]
                for component in range(3)
            ]
        )
        adjoint = solved + COURANT * (advect - couple)
        adjoint_tiles = adjoint[0].astype(jnp.bfloat16).reshape(tile_rows, 2 * levels)
        speed_tiles = stored[0].reshape(tile_rows, 2 * levels)
        picked_adjoint = jnp.take(adjoint_tiles, slot_tiles, axis=0)
        picked_speed = jnp.take(speed_tiles, slot_tiles, axis=0)
        sampled = jnp.einsum(
            "jpt,jt->jp", filters, picked_adjoint, preferred_element_type=jnp.float32
        )
        speeds = jnp.einsum("jpt,jt->jp", filters, picked_speed, preferred_element_type=jnp.float32)
        contribs = jnp.mean(speeds * speeds * sampled, axis=1)
        partial_value = jnp.sum(contribs[:, None] * matches, axis=0)
        totals = totals + lax.psum(partial_value, ("gx", "gy"))
    own_index = lax.axis_index("gx") * lax.axis_size("gy") + lax.axis_index("gy")
    owned_mask = turbine_owner == own_index
    turbine_grad = jnp.where(owned_mask, totals, jnp.float32(0.0))[None, None, :]
    return (adjoint, turbine_grad)


def solution(mesh):
    placed = (
        P(None, "gx", "gy", None),
        P(None, None, "gx", "gy", None),
        P(),
        P(),
        P("gx", "gy", None, None, None),
        P("gx", "gy", None),
        P("gx", "gy", None),
        P(),
    )
    return jax.shard_map(
        body,
        mesh=mesh,
        in_specs=placed,
        out_specs=(P(None, "gx", "gy", None), P("gx", "gy", None)),
        check_vma=False,
    )
```

profile of v0, /device:TPU:0, one launch (start us, length us, event | category | flops | bytes accessed | tf_op | source)
XLA Modules:
  0.0 101.7 jit_solution(15529138008038483000)
XLA Ops:
  0.7 0.9 fusion.126
  1.6 7.0 %collective-permute-start.5 = (bf16[4,3,1,8,256]{4,3,2,1,0:T(8,128)(2,1)S(1)}, bf16[4,3,1,8,256]{4,3,2,1,0:T(8,128)(2,1)S(1)}, u32[]{:S(2)}, u32[]{:S(2)}) collective-permute-start(bf16[4,3,1,8,256]{4,3,2,1,0:T(8,128)(2,1)S(1)} %get-tuple-element.29), channel_id=1, source_target_pairs={{2,0},{4,2},{6,4},{8,6},{10,8},{12,10},{14,12},{16,14},{18,16},{20... | collective-permute-start | bytes 147464 | tf_op jit(solution)/shard_map/ppermute | solution.py:21
  8.6 1.4 %fusion.132 = f32[192,256]{1,0:T(8,128)S(1)} fusion(f32[192,256]{1,0:T(8,128)} %bitcast.259, f32[256,256]{1,0:T(8,128)} %param.13), kind=kOutput, calls=%fused_computation.319 | convolution fusion | flops 150994944 | bytes 655360 | tf_op jit(solution)/shard_map/dot_general | solution.py:84
  10.0 5.7 %collective-permute-start = (f32[3,1,8,256]{3,2,1,0:T(8,128)S(1)}, f32[3,1,8,256]{3,2,1,0:T(8,128)S(1)}, u32[]{:S(2)}, u32[]{:S(2)}) collective-permute-start(f32[3,1,8,256]{3,2,1,0:T(8,128)S(1)} %get-tuple-element.70), channel_id=1, source_target_pairs={{2,0},{4,2},{6,4},{8,6},{10,8},{12,10},{14,12},{16,14},{18,16},{20... | collective-permute-start | bytes 73736 | tf_op jit(solution)/shard_map/ppermute | solution.py:21
  15.7 0.7 fusion.131
  24.2 0.3 fusion.39
  24.4 0.3 fusion.23
  24.9 0.5 collective-permute-start.3
  25.9 0.4 collective-permute-start.7
  26.3 0.8 collective-permute-done.6
  27.3 0.5 pad_maximum_fusion
  27.8 0.2 bitcast_convert_fusion
  28.2 0.2 fusion.21
  28.4 0.7 copy-done.1
  29.0 0.3 fusion.133
  29.5 5.6 %collective-permute-start.8 = (f32[3,1,8,256]{3,2,1,0:T(8,128)S(1)}, f32[3,1,8,256]{3,2,1,0:T(8,128)S(1)}, u32[]{:S(2)}, u32[]{:S(2)}) collective-permute-start(f32[3,1,8,256]{3,2,1,0:T(8,128)S(1)} %get-tuple-element.62), channel_id=1, source_target_pairs={{2,0},{4,2},{6,4},{8,6},{10,8},{12,10},{14,12},{16,14},{18,16},{20... | collective-permute-start | bytes 73736 | tf_op jit(solution)/shard_map/ppermute | solution.py:21
  35.1 1.8 %collective-permute-done.9 = f32[3,1,8,256]{3,2,1,0:T(8,128)S(1)} collective-permute-done((f32[3,1,8,256]{3,2,1,0:T(8,128)S(1)}, f32[3,1,8,256]{3,2,1,0:T(8,128)S(1)}, u32[]{:S(2)}, u32[]{:S(2)}) %collective-permute-start.9) | collective-permute-done | bytes 24608 | tf_op jit(solution)/shard_map/ppermute | solution.py:18
  37.0 0.5 collective-permute-start.11
  37.6 0.6 collective-permute-done.10
  38.4 0.2 fusion.29
  38.5 0.3 fusion.134
  39.0 5.7 %collective-permute-start.12 = (f32[3,1,8,256]{3,2,1,0:T(8,128)S(1)}, f32[3,1,8,256]{3,2,1,0:T(8,128)S(1)}, u32[]{:S(2)}, u32[]{:S(2)}) collective-permute-start(f32[3,1,8,256]{3,2,1,0:T(8,128)S(1)} %get-tuple-element.54), channel_id=1, source_target_pairs={{2,0},{4,2},{6,4},{8,6},{10,8},{12,10},{14,12},{16,14},{18,16},{20... | collective-permute-start | bytes 73736 | tf_op jit(solution)/shard_map/ppermute | solution.py:21
  44.8 1.7 %collective-permute-done.13 = f32[3,1,8,256]{3,2,1,0:T(8,128)S(1)} collective-permute-done((f32[3,1,8,256]{3,2,1,0:T(8,128)S(1)}, f32[3,1,8,256]{3,2,1,0:T(8,128)S(1)}, u32[]{:S(2)}, u32[]{:S(2)}) %collective-permute-start.13) | collective-permute-done | bytes 24608 | tf_op jit(solution)/shard_map/ppermute | solution.py:18
  46.6 0.5 collective-permute-start.15
  47.1 0.6 collective-permute-done.14
  47.9 0.2 fusion.37
  48.1 0.3 fusion.135
  48.5 5.7 %collective-permute-start.16 = (f32[3,1,8,256]{3,2,1,0:T(8,128)S(1)}, f32[3,1,8,256]{3,2,1,0:T(8,128)S(1)}, u32[]{:S(2)}, u32[]{:S(2)}) collective-permute-start(f32[3,1,8,256]{3,2,1,0:T(8,128)S(1)} %get-tuple-element.46), channel_id=1, source_target_pairs={{2,0},{4,2},{6,4},{8,6},{10,8},{12,10},{14,12},{16,14},{18,16},{20... | collective-permute-start | bytes 73736 | tf_op jit(solution)/shard_map/ppermute | solution.py:21
  54.3 0.6 gather_fusion
  54.9 0.6 gather_fusion.6
  55.5 0.6 gather_fusion.4
  56.1 0.6 gather_fusion.2
  56.7 0.6 gather_fusion.1
  57.3 0.6 gather_fusion.3
  58.1 0.4 collective-permute-start.19
  58.6 0.6 gather_fusion.5
  59.4 0.2 fusion.45
  59.6 0.6 gather_fusion.7
  60.3 0.2 fusion.14
  60.5 0.2 fusion.12
  60.9 0.2 fusion.10
  61.1 0.2 fusion.8
  61.5 0.2 fusion.6
  61.8 0.2 fusion.4
  62.2 0.2 fusion.2
  62.4 0.2 fusion
  62.9 38.2 %psum.34 = f32[24]{0:T(128)S(1)} all-reduce(f32[24]{0:T(128)S(1)} %add_add_fusion), channel_id=1, replica_groups=mesh['gx'=16,'gy'=2] {'gx','gy'}, use_global_device_ids=true, to_apply=%region_2.4 | all-reduce | flops 24 | bytes 192 | tf_op jit(solution)/shard_map/psum | solution.py:118
  101.1 0.5 fusion.124
  (93 shorter events, 3.5 us)
Async XLA Ops:
  0.6 59.6 %copy-start = (bf16[1,1,8,64,512]{4,3,2,1,0:T(8,128)(2,1)S(1)}, bf16[1,1,8,64,512]{4,3,2,1,0:T(8,128)(2,1)}, u32[]{:S(2)}) copy-start(bf16[1,1,8,64,512]{4,3,2,1,0:T(8,128)(2,1)} %param.14) | copy-start | bytes 1572868
  0.6 23.2 %copy-start.2 = (bf16[4,3,8,8,256]{4,3,2,1,0:T(8,128)(2,1)S(1)}, bf16[4,3,8,8,256]{4,3,2,1,0:T(8,128)(2,1)}, u32[]{:S(2)}) copy-start(bf16[4,3,8,8,256]{4,3,2,1,0:T(8,128)(2,1)} %param.11) | copy-start | bytes 1179652
  0.7 15.0 %copy-start.7 = (s32[1,1,8]{2,1,0:T(1,128)S(1)}, s32[1,1,8]{2,1,0:T(1,128)}, u32[]{:S(2)}) copy-start(s32[1,1,8]{2,1,0:T(1,128)} %param.16) | copy-start | bytes 100
  0.7 15.1 %copy-start.4 = (s32[4]{0:T(128)S(1)}, s32[4]{0:T(128)}, u32[]{:S(2)}) copy-start(s32[4]{0:T(128)} %param.12) | copy-start | bytes 52
  1.6 23.9 %collective-permute-start.5 = (bf16[4,3,1,8,256]{4,3,2,1,0:T(8,128)(2,1)S(1)}, bf16[4,3,1,8,256]{4,3,2,1,0:T(8,128)(2,1)S(1)}, u32[]{:S(2)}, u32[]{:S(2)}) collective-permute-start(bf16[4,3,1,8,256]{4,3,2,1,0:T(8,128)(2,1)S(1)} %get-tuple-element.29), channel_id=1, source_target_pairs={{2,0},{4,2},{6,4},{8,6},{10,8},{12,10},{14,12},{16,14},{18,16},{20... | collective-permute-start | bytes 147464 | tf_op jit(solution)/shard_map/ppermute | solution.py:21
  8.5 16.8 %collective-permute-start.4 = (bf16[4,3,1,8,256]{4,3,2,1,0:T(8,128)(2,1)S(1)}, bf16[4,3,1,8,256]{4,3,2,1,0:T(8,128)(2,1)S(1)}, u32[]{:S(2)}, u32[]{:S(2)}) collective-permute-start(bf16[4,3,1,8,256]{4,3,2,1,0:T(8,128)(2,1)S(1)} %get-tuple-element.30), channel_id=1, source_target_pairs={{0,2},{2,4},{4,6},{6,8},{8,10},{10,12},{12,14},{14,16},{16,18},{18... | collective-permute-start | bytes 147464 | tf_op jit(solution)/shard_map/ppermute | solution.py:18
  10.0 14.8 %collective-permute-start.1 = (f32[3,1,8,256]{3,2,1,0:T(8,128)S(1)}, f32[3,1,8,256]{3,2,1,0:T(8,128)S(1)}, u32[]{:S(2)}, u32[]{:S(2)}) collective-permute-start(f32[3,1,8,256]{3,2,1,0:T(8,128)S(1)} %get-tuple-element.69), channel_id=1, source_target_pairs={{0,2},{2,4},{4,6},{6,8},{8,10},{10,12},{12,14},{14,16},{16,18},{18... | collective-permute-start | bytes 73736 | tf_op jit(solution)/shard_map/ppermute | solution.py:18
  10.0 14.7 %collective-permute-start = (f32[3,1,8,256]{3,2,1,0:T(8,128)S(1)}, f32[3,1,8,256]{3,2,1,0:T(8,128)S(1)}, u32[]{:S(2)}, u32[]{:S(2)}) collective-permute-start(f32[3,1,8,256]{3,2,1,0:T(8,128)S(1)} %get-tuple-element.70), channel_id=1, source_target_pairs={{2,0},{4,2},{6,4},{8,6},{10,8},{12,10},{14,12},{16,14},{18,16},{20... | collective-permute-start | bytes 73736 | tf_op jit(solution)/shard_map/ppermute | solution.py:21
  24.8 3.4 %collective-permute-start.2 = (f32[3,10,1,256]{3,2,1,0:T(1,128)S(1)}, f32[3,10,1,256]{3,2,1,0:T(1,128)S(1)}, u32[]{:S(2)}, u32[]{:S(2)}) collective-permute-start(f32[3,10,1,256]{3,2,1,0:T(1,128)S(1)} %get-tuple-element.37), channel_id=1, source_target_pairs={{1,0},{0,1},{3,2},{2,3},{5,4},{4,5},{7,6},{6,7},{9,8},{8,9},{11,10... | collective-permute-start | bytes 92168 | tf_op jit(solution)/shard_map/ppermute | solution.py:21
  24.9 3.3 %collective-permute-start.3 = (f32[3,10,1,256]{3,2,1,0:T(1,128)S(1)}, f32[3,10,1,256]{3,2,1,0:T(1,128)S(1)}, u32[]{:S(2)}, u32[]{:S(2)}) collective-permute-start(f32[3,10,1,256]{3,2,1,0:T(1,128)S(1)} %get-tuple-element.38), channel_id=1, source_target_pairs={{0,1},{1,0},{2,3},{3,2},{4,5},{5,4},{6,7},{7,6},{8,9},{9,8},{10,11... | collective-permute-start | bytes 92168 | tf_op jit(solution)/shard_map/ppermute | solution.py:18
  25.7 1.4 %collective-permute-start.6 = (bf16[4,3,10,1,256]{4,3,2,1,0:T(2,128)(2,1)S(1)}, bf16[4,3,10,1,256]{4,3,2,1,0:T(2,128)(2,1)S(1)}, u32[]{:S(2)}, u32[]{:S(2)}) collective-permute-start(bf16[4,3,10,1,256]{4,3,2,1,0:T(2,128)(2,1)S(1)} %get-tuple-element.15), channel_id=1, source_target_pairs={{0,1},{1,0},{2,3},{3,2},{4,5},{5,4},{6,7},{7,6},{8,9},{9,8},{10,11... | collective-permute-start | bytes 184328 | tf_op jit(solution)/shard_map/ppermute | solution.py:18
  25.9 1.4 %collective-permute-start.7 = (bf16[4,3,10,1,256]{4,3,2,1,0:T(2,128)(2,1)S(1)}, bf16[4,3,10,1,256]{4,3,2,1,0:T(2,128)(2,1)S(1)}, u32[]{:S(2)}, u32[]{:S(2)}) collective-permute-start(bf16[4,3,10,1,256]{4,3,2,1,0:T(2,128)(2,1)S(1)} %get-tuple-element.16), channel_id=1, source_target_pairs={{1,0},{0,1},{3,2},{2,3},{5,4},{4,5},{7,6},{6,7},{9,8},{8,9},{11,10... | collective-permute-start | bytes 184328 | tf_op jit(solution)/shard_map/ppermute | solution.py:21
  28.1 1.0 copy-start.1
  29.4 7.5 %collective-permute-start.9 = (f32[3,1,8,256]{3,2,1,0:T(8,128)S(1)}, f32[3,1,8,256]{3,2,1,0:T(8,128)S(1)}, u32[]{:S(2)}, u32[]{:S(2)}) collective-permute-start(f32[3,1,8,256]{3,2,1,0:T(8,128)S(1)} %get-tuple-element.61), channel_id=1, source_target_pairs={{0,2},{2,4},{4,6},{6,8},{8,10},{10,12},{12,14},{14,16},{16,18},{18... | collective-permute-start | bytes 73736 | tf_op jit(solution)/shard_map/ppermute | solution.py:18
  29.5 7.4 %collective-permute-start.8 = (f32[3,1,8,256]{3,2,1,0:T(8,128)S(1)}, f32[3,1,8,256]{3,2,1,0:T(8,128)S(1)}, u32[]{:S(2)}, u32[]{:S(2)}) collective-permute-start(f32[3,1,8,256]{3,2,1,0:T(8,128)S(1)} %get-tuple-element.62), channel_id=1, source_target_pairs={{2,0},{4,2},{6,4},{8,6},{10,8},{12,10},{14,12},{16,14},{18,16},{20... | collective-permute-start | bytes 73736 | tf_op jit(solution)/shard_map/ppermute | solution.py:21
  36.9 1.3 %collective-permute-start.10 = (f32[3,10,1,256]{3,2,1,0:T(1,128)S(1)}, f32[3,10,1,256]{3,2,1,0:T(1,128)S(1)}, u32[]{:S(2)}, u32[]{:S(2)}) collective-permute-start(f32[3,10,1,256]{3,2,1,0:T(1,128)S(1)} %get-tuple-element.35), channel_id=1, source_target_pairs={{1,0},{0,1},{3,2},{2,3},{5,4},{4,5},{7,6},{6,7},{9,8},{8,9},{11,10... | collective-permute-start | bytes 92168 | tf_op jit(solution)/shard_map/ppermute | solution.py:21
  37.0 1.4 %collective-permute-start.11 = (f32[3,10,1,256]{3,2,1,0:T(1,128)S(1)}, f32[3,10,1,256]{3,2,1,0:T(1,128)S(1)}, u32[]{:S(2)}, u32[]{:S(2)}) collective-permute-start(f32[3,10,1,256]{3,2,1,0:T(1,128)S(1)} %get-tuple-element.36), channel_id=1, source_target_pairs={{0,1},{1,0},{2,3},{3,2},{4,5},{5,4},{6,7},{7,6},{8,9},{9,8},{10,11... | collective-permute-start | bytes 92168 | tf_op jit(solution)/shard_map/ppermute | solution.py:18
  38.9 7.6 %collective-permute-start.13 = (f32[3,1,8,256]{3,2,1,0:T(8,128)S(1)}, f32[3,1,8,256]{3,2,1,0:T(8,128)S(1)}, u32[]{:S(2)}, u32[]{:S(2)}) collective-permute-start(f32[3,1,8,256]{3,2,1,0:T(8,128)S(1)} %get-tuple-element.53), channel_id=1, source_target_pairs={{0,2},{2,4},{4,6},{6,8},{8,10},{10,12},{12,14},{14,16},{16,18},{18... | collective-permute-start | bytes 73736 | tf_op jit(solution)/shard_map/ppermute | solution.py:18
  39.0 7.5 %collective-permute-start.12 = (f32[3,1,8,256]{3,2,1,0:T(8,128)S(1)}, f32[3,1,8,256]{3,2,1,0:T(8,128)S(1)}, u32[]{:S(2)}, u32[]{:S(2)}) collective-permute-start(f32[3,1,8,256]{3,2,1,0:T(8,128)S(1)} %get-tuple-element.54), channel_id=1, source_target_pairs={{2,0},{4,2},{6,4},{8,6},{10,8},{12,10},{14,12},{16,14},{18,16},{20... | collective-permute-start | bytes 73736 | tf_op jit(solution)/shard_map/ppermute | solution.py:21
  46.5 1.3 %collective-permute-start.14 = (f32[3,10,1,256]{3,2,1,0:T(1,128)S(1)}, f32[3,10,1,256]{3,2,1,0:T(1,128)S(1)}, u32[]{:S(2)}, u32[]{:S(2)}) collective-permute-start(f32[3,10,1,256]{3,2,1,0:T(1,128)S(1)} %get-tuple-element.33), channel_id=1, source_target_pairs={{1,0},{0,1},{3,2},{2,3},{5,4},{4,5},{7,6},{6,7},{9,8},{8,9},{11,10... | collective-permute-start | bytes 92168 | tf_op jit(solution)/shard_map/ppermute | solution.py:21
  46.6 1.4 %collective-permute-start.15 = (f32[3,10,1,256]{3,2,1,0:T(1,128)S(1)}, f32[3,10,1,256]{3,2,1,0:T(1,128)S(1)}, u32[]{:S(2)}, u32[]{:S(2)}) collective-permute-start(f32[3,10,1,256]{3,2,1,0:T(1,128)S(1)} %get-tuple-element.34), channel_id=1, source_target_pairs={{0,1},{1,0},{2,3},{3,2},{4,5},{5,4},{6,7},{7,6},{8,9},{9,8},{10,11... | collective-permute-start | bytes 92168 | tf_op jit(solution)/shard_map/ppermute | solution.py:18
  48.5 9.4 %collective-permute-start.17 = (f32[3,1,8,256]{3,2,1,0:T(8,128)S(1)}, f32[3,1,8,256]{3,2,1,0:T(8,128)S(1)}, u32[]{:S(2)}, u32[]{:S(2)}) collective-permute-start(f32[3,1,8,256]{3,2,1,0:T(8,128)S(1)} %get-tuple-element.45), channel_id=1, source_target_pairs={{0,2},{2,4},{4,6},{6,8},{8,10},{10,12},{12,14},{14,16},{16,18},{18... | collective-permute-start | bytes 73736 | tf_op jit(solution)/shard_map/ppermute | solution.py:18
  48.5 9.4 %collective-permute-start.16 = (f32[3,1,8,256]{3,2,1,0:T(8,128)S(1)}, f32[3,1,8,256]{3,2,1,0:T(8,128)S(1)}, u32[]{:S(2)}, u32[]{:S(2)}) collective-permute-start(f32[3,1,8,256]{3,2,1,0:T(8,128)S(1)} %get-tuple-element.46), channel_id=1, source_target_pairs={{2,0},{4,2},{6,4},{8,6},{10,8},{12,10},{14,12},{16,14},{18,16},{20... | collective-permute-start | bytes 73736 | tf_op jit(solution)/shard_map/ppermute | solution.py:21
  58.0 1.3 %collective-permute-start.18 = (f32[3,10,1,256]{3,2,1,0:T(1,128)S(1)}, f32[3,10,1,256]{3,2,1,0:T(1,128)S(1)}, u32[]{:S(2)}, u32[]{:S(2)}) collective-permute-start(f32[3,10,1,256]{3,2,1,0:T(1,128)S(1)} %get-tuple-element.31), channel_id=1, source_target_pairs={{1,0},{0,1},{3,2},{2,3},{5,4},{4,5},{7,6},{6,7},{9,8},{8,9},{11,10... | collective-permute-start | bytes 92168 | tf_op jit(solution)/shard_map/ppermute | solution.py:21
  58.1 1.3 %collective-permute-start.19 = (f32[3,10,1,256]{3,2,1,0:T(1,128)S(1)}, f32[3,10,1,256]{3,2,1,0:T(1,128)S(1)}, u32[]{:S(2)}, u32[]{:S(2)}) collective-permute-start(f32[3,10,1,256]{3,2,1,0:T(1,128)S(1)} %get-tuple-element.32), channel_id=1, source_target_pairs={{0,1},{1,0},{2,3},{3,2},{4,5},{5,4},{6,7},{7,6},{8,9},{9,8},{10,11... | collective-permute-start | bytes 92168 | tf_op jit(solution)/shard_map/ppermute | solution.py:18
  59.6 1.6 %copy-start.3 = (f32[3,8,8,256]{3,2,1,0:T(8,128)}, f32[3,8,8,256]{3,2,1,0:T(8,128)S(1)}, u32[]{:S(2)}) copy-start(f32[3,8,8,256]{3,2,1,0:T(8,128)S(1)} %fusion.45) | copy-start | bytes 589828
  61.8 1.0 %copy-start.5 = (s32[1,1,8]{2,1,0:T(1,128)S(1)}, s32[1,1,8]{2,1,0:T(1,128)}, u32[]{:S(2)}) copy-start(s32[1,1,8]{2,1,0:T(1,128)} %param.15) | copy-start | bytes 100
  61.8 39.4 %copy-start.6 = (s32[24]{0:T(128)S(1)}, s32[24]{0:T(128)}, u32[]{:S(2)}) copy-start(s32[24]{0:T(128)} %param.17) | copy-start | bytes 292
where the time goes:
time: 102 us
  blocking collectives  38.2 us (37%)
  starting transfers between devices  32.8 us (32%)
  between operations  8.73 us (9%)
  local copies, waits for them, and re-layouts  7.24 us (7%)
  waiting for transfers between devices  6.22 us (6%)
  matrix products  4.3 us (4%)
  other arithmetic  4.12 us (4%)
    psum x1, blocking collectives, body(): totals = totals + lax.psum(partial_value, ('gx', 'gy'))  38.2 us
    ppermute x10, starting transfers between devices, extended(): lax.ppermute(lax.slice_in_dim(block, 0, width, axis=dim), axis, backward)  30.5 us
    ppermute x10, waiting for transfers between devices, extended(): lax.ppermute(lax.slice_in_dim(block, block.shape[dim] - width, None, axis...  4.73 us
    dot_general x4, matrix products, body(): jnp.dot(adjoint.reshape(-1, levels), vertical_inverse, precision=lax.Prec...  2.37 us
    ppermute x10, starting transfers between devices, extended(): lax.ppermute(lax.slice_in_dim(block, block.shape[dim] - width, None, axis...  2.31 us
    gather x4, local copies, waits for them, and re-layouts, body(): picked_speed = jnp.take(speed_tiles, slot_tiles, axis=0)  2.28 us
    gather x4, local copies, waits for them, and re-layouts, body(): picked_adjoint = jnp.take(adjoint_tiles, slot_tiles, axis=0)  2.28 us
  transfers between devices with their start and end apart: 20, of which 9 were waited for; matrix products, arithmetic and copies ran while one was open for 8% of the time, Pallas kernels for 0%

commit v1 on v0

v1 whole, which is shorter than its diff:
```python
import functools

import jax
import jax.numpy as jnp
from jax import lax
from jax.experimental import pallas as pl
from jax.experimental.pallas import tpu as pltpu
from jax.sharding import PartitionSpec as P

COURANT = 0.2
HALF = 0.5 * COURANT
MESH = pl.DeviceIdType.MESH
F32 = jnp.float32
BF16 = jnp.bfloat16


def pack(rows):
    parts = [rows[:, k : k + 128] for k in range(0, rows.shape[1], 128)]
    return jnp.concatenate(parts, axis=0).astype(BF16)


def unpack(packed, count):
    wide = packed.astype(F32)
    return jnp.concatenate(
        [wide[k : k + count] for k in range(0, wide.shape[0], count)], axis=1
    )


def read(view, rows):
    return jnp.concatenate([view[k, rows, :] for k in range(view.shape[0])], axis=1)


def write(view, rows, value):
    for k in range(view.shape[0]):
        view[k, rows, :] = value[:, 128 * k : 128 * (k + 1)]


def stream_diff(f):
    zero = jnp.zeros_like(f[:1])
    return jnp.concatenate([f[1:], zero], axis=0) - jnp.concatenate([zero, f[:-1]], axis=0)


def rolled_diff(f, axis):
    size = f.shape[axis]
    place = lax.broadcasted_iota(jnp.int32, f.shape, axis)
    above = jnp.where(place == size - 1, 0.0, pltpu.roll(f, size - 1, axis))
    below = jnp.where(place == 0, 0.0, pltpu.roll(f, 1, axis))
    return above - below


def kernel(
    dims,
    init_hbm, states_hbm, index_hbm, inverse_hbm, filter_hbm, turbine_hbm, tile_hbm, owner_hbm,
    out_hbm, grad_ref,
    adj, states, index_s, inverse, filters, turbine_s, tile_s, owner_s,
    inv_hi, inv_lo, solved, vel, history,
    send_v, recv_v, send_s, recv_s,
    part_y, got_y, part_x, got_x,
    load_sem, out_sem, sv_sem, rv_sem, ss_sem, rs_sem, sy_sem, ry_sem, sx_sem, rx_sem,
):
    ngx, ngy, comps, sx, sy, steps, slots, points, turbines = dims
    cols = sx * sy
    halves = adj.shape[0]
    levels = 128 * halves
    everything = pl.ds(0, comps * cols)
    gx, gy = lax.axis_index("gx"), lax.axis_index("gy")

    loads = [
        pltpu.make_async_copy(src, dst, load_sem.at[k])
        for k, (src, dst) in enumerate((
            (index_hbm, index_s), (states_hbm, states), (inverse_hbm, inverse),
            (turbine_hbm, turbine_s), (tile_hbm, tile_s), (owner_hbm, owner_s), (filter_hbm, filters),
            *((init_hbm.at[:, pl.ds(128 * k, 128)], adj.at[k]) for k in range(halves)),
        ))
    ]
    for load in loads:
        load.start()

    barrier = pltpu.get_barrier_semaphore()

    def greet_x(k, c):
        pl.semaphore_signal(barrier, inc=1, device_id=(lax.rem(gx + k, ngx), gy), device_id_type=MESH)
        return c

    def greet_y(k, c):
        pl.semaphore_signal(barrier, inc=1, device_id=(gx, lax.rem(gy + k, ngy)), device_id_type=MESH)
        return c

    lax.fori_loop(1, ngx, greet_x, 0)
    lax.fori_loop(1, ngy, greet_y, 0)

    beside = (
        (lax.rem(gx + ngx - 1, ngx), gy),
        (lax.rem(gx + 1, ngx), gy),
        (gx, lax.rem(gy + ngy - 1, ngy)),
        (gx, lax.rem(gy + 1, ngy)),
    )

    def edge(c, side):
        base = c * cols
        if side == 0:
            return pl.ds(base, sy)
        if side == 1:
            return pl.ds(base + cols - sy, sy)
        return pl.ds(base + (0 if side == 2 else sy - 1), sx, stride=sy)

    def take(view, c, side):
        return read(view, edge(c, side))

    def put(view, c, side, value):
        write(view, edge(c, side), value)

    def stage(view, staging, s):
        for side in range(4):
            staging[s, side] = pack(
                jnp.concatenate([take(view, c, side) for c in range(comps)], axis=0)
            )

    def copy(staging, landing, ssem, rsem, s, side):
        return pltpu.make_async_remote_copy(
            src_ref=staging.at[s, side],
            dst_ref=landing.at[s, side ^ 1],
            send_sem=ssem.at[s, side],
            recv_sem=rsem.at[s, side ^ 1],
            device_id=beside[side],
            device_id_type=MESH,
        )

    def copies(*refs):
        return [copy(*refs, side) for side in range(4)]

    def prepare(s):
        write(vel.at[s], everything, states[index_s[s]].astype(F32))
        stage(vel.at[s], send_v, s)

    def solve(s):
        value = read(adj, everything)
        hi = value.astype(BF16)
        lo = (value - hi.astype(F32)).astype(BF16)
        dot = functools.partial(jnp.dot, preferred_element_type=F32)
        product = dot(hi, inv_hi[...]) + (dot(hi, inv_lo[...]) + dot(lo, inv_hi[...]))
        write(solved, everything, product)
        stage(solved, send_s, s)

    loads[2].wait()
    whole = inverse[...]
    high = whole.astype(BF16)
    inv_hi[...] = high
    inv_lo[...] = (whole - high.astype(F32)).astype(BF16)
    for load in loads[7:]:
        load.wait()
    solve(0)
    loads[0].wait()
    loads[1].wait()
    prepare(0)

    pl.semaphore_wait(barrier, ngx - 1 + ngy - 1)
    for sent in copies(send_v, recv_v, sv_sem, rv_sem, 0):
        sent.start()

    def step(s, carry):
        for sent in copies(send_s, recv_s, ss_sem, rs_sem, s):
            sent.start()

        @pl.when(s < steps - 1)
        def _():
            prepare(s + 1)
            for sent in copies(send_v, recv_v, sv_sem, rv_sem, s + 1):
                sent.start()

        blocks = lambda view, c: read(view, pl.ds(c * cols, cols)).reshape(sx, sy, levels)
        speed = [blocks(vel.at[s], c) for c in range(comps)]
        differences = (
            stream_diff,
            lambda f: rolled_diff(f, 1),
            lambda f: rolled_diff(f, 2),
        )
        current = [blocks(solved, c) for c in range(comps)]
        for c in range(comps):
            total = 0.0
            for d in range(comps):
                total = total + speed[d] * differences[d](current[c])
                total = total - current[d] * differences[c](speed[d])
            write(adj, pl.ds(c * cols, cols), (current[c] + HALF * total).reshape(cols, levels))

        for side in range(4):
            copy(send_v, recv_v, sv_sem, rv_sem, s, side ^ 1).wait_recv()
            copy(send_s, recv_s, ss_sem, rs_sem, s, side ^ 1).wait_recv()
            sign = -HALF if side % 2 == 0 else HALF
            across = side // 2
            width = sy if across == 0 else sx
            far = unpack(recv_s[s, side], comps * width)
            far_speed = unpack(recv_v[s, side], comps * width)
            carrier = sign * take(vel.at[s], across, side)
            for c in range(comps):
                new = take(adj, c, side) + carrier * far[c * width : (c + 1) * width]
                if c == across:
                    couple = 0.0
                    for d in range(comps):
                        couple = couple + take(solved, d, side) * far_speed[d * width : (d + 1) * width]
                    new = new - sign * couple
                put(adj, c, side, new)

        history[s] = read(adj, pl.ds(0, cols)).astype(BF16)

        @pl.when(s < steps - 1)
        def _():
            solve(s + 1)

        return carry

    lax.fori_loop(0, steps, step, 0)

    outs = [
        pltpu.make_async_copy(adj.at[k], out_hbm.at[:, pl.ds(128 * k, 128)], out_sem.at[k])
        for k in range(halves)
    ]
    for out in outs:
        out.start()

    for load in loads[3:6]:
        load.wait()
    rows = lax.broadcasted_iota(jnp.int32, (2 * slots, cols), 0)
    places = lax.broadcasted_iota(jnp.int32, (2 * slots, cols), 1)
    wanted = jnp.zeros((2 * slots, cols), jnp.int32)
    lanes = got_x.shape[-1]
    slot_rows = lax.broadcasted_iota(jnp.int32, (slots, lanes), 0)
    lane = lax.broadcasted_iota(jnp.int32, (slots, lanes), 1)
    named = jnp.full((slots, lanes), turbines, jnp.int32)
    for j in range(slots):
        first = 2 * tile_s[0, 0, j]
        wanted = jnp.where(rows == j, first, wanted)
        wanted = jnp.where(rows == slots + j, first + 1, wanted)
        named = jnp.where(slot_rows == j, turbine_s[0, 0, j], named)
    pick = jnp.where(wanted == places, 1.0, 0.0).astype(BF16)
    sources = [history[s] for s in range(steps)]
    sources += [read(vel.at[s], pl.ds(0, cols)).astype(BF16) for s in range(steps)]
    vectors = []
    for source in sources:
        picked = jnp.dot(pick, source, preferred_element_type=F32)
        vectors.append(jnp.concatenate([picked[:slots], picked[slots:]], axis=1))
    stacked = jnp.concatenate(vectors, axis=0).astype(BF16)
    loads[6].wait()
    seen = lax.dot_general(
        stacked, filters[...], (((1,), (1,)), ((), ())), preferred_element_type=F32
    )
    terms = 0.0
    for s in range(steps):
        sampled = seen[s * slots : (s + 1) * slots]
        speeds = seen[(steps + s) * slots : (steps + s + 1) * slots]
        terms = terms + speeds * speeds * sampled
    owner_row = lax.broadcasted_iota(jnp.int32, terms.shape, 0)
    owner_col = lax.broadcasted_iota(jnp.int32, terms.shape, 1)
    start = owner_row * points
    inside = (owner_col >= start) & (owner_col < start + points)
    term = jnp.sum(jnp.where(inside, terms, 0.0), axis=1, keepdims=True) * (1.0 / points)
    live = (named == lane) & (lane < turbines)
    part_y[...] = jnp.sum(jnp.where(live, term, 0.0), axis=0, keepdims=True)

    def span_copy(k):
        return pltpu.make_async_remote_copy(
            src_ref=part_y, dst_ref=got_y.at[k - 1],
            send_sem=sy_sem.at[k - 1], recv_sem=ry_sem.at[k - 1],
            device_id=(gx, lax.rem(gy + k, ngy)), device_id_type=MESH,
        )

    def stream_copy(k):
        return pltpu.make_async_remote_copy(
            src_ref=part_x, dst_ref=got_x.at[k - 1],
            send_sem=sx_sem.at[k - 1], recv_sem=rx_sem.at[k - 1],
            device_id=(lax.rem(gx + k, ngx), gy), device_id_type=MESH,
        )

    def run(make, count, act):
        def one(k, c):
            act(make(k))
            return c
        lax.fori_loop(1, count, one, 0)

    run(span_copy, ngy, lambda c: c.start())
    run(span_copy, ngy, lambda c: c.wait_recv())
    part_x[...] = part_y[...] + jnp.sum(got_y[...], axis=0)
    run(stream_copy, ngx, lambda c: c.start())
    mine = jnp.zeros((1, lanes), jnp.int32) - 1
    lane_row = lax.broadcasted_iota(jnp.int32, (1, lanes), 1)
    for t in range(turbines):
        mine = jnp.where(lane_row == t, owner_s[t], mine)
    run(stream_copy, ngx, lambda c: c.wait_recv())
    summed = part_x[...] + jnp.sum(got_x[...], axis=0)
    grad = jnp.where(mine == gx * ngy + gy, summed, 0.0)
    grad_ref[...] = grad[:, :turbines].reshape(grad_ref.shape)

    def drain(s, c):
        for sent in copies(send_v, recv_v, sv_sem, rv_sem, s):
            sent.wait_send()
        for sent in copies(send_s, recv_s, ss_sem, rs_sem, s):
            sent.wait_send()
        return c

    lax.fori_loop(0, steps, drain, 0)
    run(span_copy, ngy, lambda c: c.wait_send())
    run(stream_copy, ngx, lambda c: c.wait_send())
    for out in outs:
        out.wait()


def body(sizes, adjoint_init, saved_states, step_index, vertical_inverse, disk_filter,
         pair_turbine, pair_tile, turbine_owner):
    ngx, ngy = sizes
    comps, sx, sy, levels = adjoint_init.shape
    saved = saved_states.shape[0]
    steps = step_index.shape[0]
    slots, points, cells = disk_filter.shape[2:]
    turbines = turbine_owner.shape[0]
    rows = comps * sx * sy
    lanes = -(-turbines // 128) * 128
    packed = comps * max(sx, sy) * levels // 128
    halves = levels // 128
    dims = (ngx, ngy, comps, sx, sy, steps, slots, points, turbines)
    anywhere = pl.BlockSpec(memory_space=pl.ANY)
    halo = pltpu.VMEM((steps, 4, packed, 128), BF16)
    dma = pltpu.SemaphoreType.DMA
    final, grad = pl.pallas_call(
        functools.partial(kernel, dims),
        out_shape=(
            jax.ShapeDtypeStruct((rows, levels), F32),
            jax.ShapeDtypeStruct((1, 1, turbines), F32),
        ),
        in_specs=[anywhere] * 8,
        out_specs=(anywhere, pl.BlockSpec(memory_space=pltpu.VMEM)),
        scratch_shapes=[
            pltpu.VMEM((halves, rows, 128), F32),
            pltpu.VMEM((saved, rows, levels), BF16),
            pltpu.SMEM(step_index.shape, jnp.int32),
            pltpu.VMEM((levels, levels), F32),
            pltpu.VMEM((slots * points, cells), BF16),
            pltpu.SMEM(pair_turbine.shape, jnp.int32),
            pltpu.SMEM(pair_tile.shape, jnp.int32),
            pltpu.SMEM(turbine_owner.shape, jnp.int32),
            pltpu.VMEM((levels, levels), BF16),
            pltpu.VMEM((levels, levels), BF16),
            pltpu.VMEM((halves, rows, 128), F32),
            pltpu.VMEM((steps, halves, rows, 128), F32),
            pltpu.VMEM((steps, sx * sy, levels), BF16),
            halo, halo, halo, halo,
            pltpu.VMEM((1, lanes), F32),
            pltpu.VMEM((ngy - 1, 1, lanes), F32),
            pltpu.VMEM((1, lanes), F32),
            pltpu.VMEM((ngx - 1, 1, lanes), F32),
            dma((7 + halves,)), dma((halves,)),
            dma((steps, 4)), dma((steps, 4)), dma((steps, 4)), dma((steps, 4)),
            dma((ngy - 1,)), dma((ngy - 1,)), dma((ngx - 1,)), dma((ngx - 1,)),
        ],
        compiler_params=pltpu.CompilerParams(
            collective_id=0, has_side_effects=True, vmem_limit_bytes=48 * 1024 * 1024
        ),
        name="sweep",
    )(
        adjoint_init.reshape(rows, levels),
        saved_states.reshape(saved, rows, levels),
        step_index,
        vertical_inverse,
        disk_filter.reshape(slots * points, cells),
        pair_turbine,
        pair_tile,
        turbine_owner,
    )
    return final.reshape(adjoint_init.shape), grad


def solution(mesh):
    placed = (
        P(None, "gx", "gy", None),
        P(None, None, "gx", "gy", None),
        P(),
        P(),
        P("gx", "gy", None, None, None),
        P("gx", "gy", None),
        P("gx", "gy", None),
        P(),
    )
    return jax.shard_map(
        functools.partial(body, (mesh.shape["gx"], mesh.shape["gy"])),
        mesh=mesh,
        in_specs=placed,
        out_specs=(P(None, "gx", "gy", None), P("gx", "gy", None)),
        check_vma=False,
    )
```

time: 102 us -> 37 us (0.36)
  blocking collectives: 38.2 us -> 0 us
  starting transfers between devices: 32.8 us -> 0 us
  Pallas kernels: 0 us -> 30.3 us
  between operations: 8.73 us -> 0.68 us
  waiting for transfers between devices: 6.22 us -> 0 us
  matrix products: 4.3 us -> 0 us
  other arithmetic: 4.12 us -> 0 us
  local copies, waits for them, and re-layouts: 7.24 us -> 5.77 us
    psum x1 -> x0, blocking collectives: 38.2 us -> none  [body(): totals = totals + lax.psum(partial_value, ('gx', 'gy'))]
    ppermute x20 -> x0, starting transfers between devices: 32.8 us -> none  [the longest x10 30.5 us: extended(): lax.ppermute(lax.slice_in_dim(block, 0, width, axis=dim), axis, backward)]
    pallas_call x0 -> x1, Pallas kernels: none -> 30.3 us  [body(): pl.pallas_call(functools.partial(kernel, dims), out_shape=(jax.ShapeDtype...]
    ppermute x20 -> x0, waiting for transfers between devices: 6.22 us -> none  [the longest x10 4.73 us: extended(): lax.ppermute(lax.slice_in_dim(block, block.shape[dim] - width, None, axis...]
    unnamed x18, local copies, waits for them, and re-layouts: 0.73 us -> 5.77 us
    gather x8 -> x0, local copies, waits for them, and re-layouts: 4.57 us -> none  [the longest x4 2.28 us: body(): picked_speed = jnp.take(speed_tiles, slot_tiles, axis=0)]
    dot_general x12 -> x0, matrix products: 4.3 us -> none  [the longest x4 2.37 us: body(): jnp.dot(adjoint.reshape(-1, levels), vertical_inverse, precision=lax.Prec...]
    slice x12 -> x0, local copies, waits for them, and re-layouts: 1.8 us -> none  [the longest x1 0.91 us: extended(): lax.slice_in_dim(block, 0, width, axis=dim)]
  transfers between devices with their start and end apart: 20 -> 0, of which waited for: 9 -> 0; matrix products, arithmetic and copies ran while one was open for 8% -> 0% of each run, Pallas kernels for 0% -> 0%
where the time goes in v1:
time: 37 us; the launch traced here: 36.8 us
  Pallas kernels  30.3 us (82%)
  local copies, waits for them, and re-layouts  5.77 us (16%)
  between operations  0.68 us (2%)
    pallas_call x1, Pallas kernels, body(): pl.pallas_call(functools.partial(kernel, dims), out_shape=(jax.ShapeDtype...  30.3 us
    unnamed x18, local copies, waits for them, and re-layouts  5.77 us

profile of v1, /device:TPU:0, one launch (start us, length us, event | category | flops | bytes accessed | tf_op | source)
XLA Modules:
  0.0 36.8 jit_solution(4796892027974044032)
XLA Ops:
  0.6 0.0 copy-start.7
  0.6 0.0 copy-start.4
  0.7 0.0 copy-start.5
  0.7 0.0 copy-start.6
  0.7 0.6 %copy-done.7 = s32[24]{0:T(128)S(1)} copy-done((s32[24]{0:T(128)S(1)}, s32[24]{0:T(128)}, u32[]{:S(2)}) %copy-start.7) | copy-done | bytes 120
  1.3 0.0 copy-done.4
  1.3 0.0 copy-done.5
  1.3 0.0 copy-done.6
  1.3 0.0 copy-start
  1.3 1.0 %copy-done = bf16[1,1,8,64,512]{4,3,2,1,0:T(8,128)(2,1)S(1)} copy-done((bf16[1,1,8,64,512]{4,3,2,1,0:T(8,128)(2,1)S(1)}, bf16[1,1,8,64,512]{4,3,2,1,0:T(8,128)(2,1)}, u32[]{:S(2)}) %copy-start) | copy-done | bytes 524312
  2.4 0.0 copy-start.1
  2.4 1.0 %copy-done.1 = bf16[4,3,8,8,256]{4,3,2,1,0:T(8,128)(2,1)S(1)} copy-done((bf16[4,3,8,8,256]{4,3,2,1,0:T(8,128)(2,1)S(1)}, bf16[4,3,8,8,256]{4,3,2,1,0:T(8,128)(2,1)}, u32[]{:S(2)}) %copy-start.1) | copy-done | bytes 393240
  3.4 0.0 copy-start.2
  3.4 0.9 %copy-done.2 = f32[256,256]{1,0:T(8,128)S(1)} copy-done((f32[256,256]{1,0:T(8,128)S(1)}, f32[256,256]{1,0:T(8,128)}, u32[]{:S(2)}) %copy-start.2) | copy-done | bytes 262168
  4.3 0.0 copy-start.3
  4.3 0.9 %copy-done.3 = f32[3,8,8,256]{3,2,1,0:T(8,128)S(1)} copy-done((f32[3,8,8,256]{3,2,1,0:T(8,128)S(1)}, f32[3,8,8,256]{3,2,1,0:T(8,128)}, u32[]{:S(2)}) %copy-start.3) | copy-done | bytes 196632
  5.3 30.3 %sweep.1 = (f32[192,256]{1,0:T(8,128)S(1)}, f32[1,1,24]{2,1,0:T(1,128)S(1)}) custom-call(f32[192,256]{1,0:T(8,128)S(1)} %bitcast.7, bf16[4,192,256]{2,1,0:T(8,128)(2,1)S(1)} %bitcast.5, s32[4]{0:T(128)S(1)} %copy-done.4, f32[256,256]{1,0:T(8,128)S(1)} %copy-done.2, bf16[512,512]{1,0:T(8,128)(2,1)S(1)} %bitcast.4, s32[1,1,8]{2,1,0:T(1,128)S(1)} %copy-done.5, ...), custom_call_target="tpu_custom_call" | custom-call | tf_op jit(solution)/shard_map/sweep/pallas_call | solution.py:323
  35.6 0.7 %copy.12 = f32[3,8,8,256]{3,2,1,0:T(8,128)} copy(f32[3,8,8,256]{3,2,1,0:T(8,128)S(1)} %bitcast.6) | data formatting | bytes 393216
  36.3 0.5 %copy.13 = f32[1,1,24]{2,1,0:T(1,128)} copy(f32[1,1,24]{2,1,0:T(1,128)S(1)} %get-tuple-element.9) | data formatting | bytes 192
Async XLA Ops:
  0.6 0.7 %copy-start.7 = (s32[24]{0:T(128)S(1)}, s32[24]{0:T(128)}, u32[]{:S(2)}) copy-start(s32[24]{0:T(128)} %owner_hbm.1) | copy-start | bytes 292
  0.6 0.7 %copy-start.4 = (s32[4]{0:T(128)S(1)}, s32[4]{0:T(128)}, u32[]{:S(2)}) copy-start(s32[4]{0:T(128)} %index_hbm.1) | copy-start | bytes 52
  0.7 0.7 %copy-start.5 = (s32[1,1,8]{2,1,0:T(1,128)S(1)}, s32[1,1,8]{2,1,0:T(1,128)}, u32[]{:S(2)}) copy-start(s32[1,1,8]{2,1,0:T(1,128)} %turbine_hbm.1) | copy-start | bytes 100
  0.7 0.7 %copy-start.6 = (s32[1,1,8]{2,1,0:T(1,128)S(1)}, s32[1,1,8]{2,1,0:T(1,128)}, u32[]{:S(2)}) copy-start(s32[1,1,8]{2,1,0:T(1,128)} %tile_hbm.1) | copy-start | bytes 100
  1.3 1.0 %copy-start = (bf16[1,1,8,64,512]{4,3,2,1,0:T(8,128)(2,1)S(1)}, bf16[1,1,8,64,512]{4,3,2,1,0:T(8,128)(2,1)}, u32[]{:S(2)}) copy-start(bf16[1,1,8,64,512]{4,3,2,1,0:T(8,128)(2,1)} %param.12) | copy-start | bytes 1572868
  2.4 1.0 %copy-start.1 = (bf16[4,3,8,8,256]{4,3,2,1,0:T(8,128)(2,1)S(1)}, bf16[4,3,8,8,256]{4,3,2,1,0:T(8,128)(2,1)}, u32[]{:S(2)}) copy-start(bf16[4,3,8,8,256]{4,3,2,1,0:T(8,128)(2,1)} %param.9) | copy-start | bytes 1179652
  3.4 0.9 %copy-start.2 = (f32[256,256]{1,0:T(8,128)S(1)}, f32[256,256]{1,0:T(8,128)}, u32[]{:S(2)}) copy-start(f32[256,256]{1,0:T(8,128)} %inverse_hbm.1) | copy-start | bytes 786436
  4.3 0.9 %copy-start.3 = (f32[3,8,8,256]{3,2,1,0:T(8,128)S(1)}, f32[3,8,8,256]{3,2,1,0:T(8,128)}, u32[]{:S(2)}) copy-start(f32[3,8,8,256]{3,2,1,0:T(8,128)} %param.8) | copy-start | bytes 589828

commit v2 on v1

v2 whole, which is shorter than its diff:
```python
import functools

import jax
import jax.numpy as jnp
from jax import lax
from jax.experimental import pallas as pl
from jax.experimental.pallas import tpu as pltpu
from jax.sharding import PartitionSpec as P

COURANT = 0.2
HALF = 0.5 * COURANT
MESH = pl.DeviceIdType.MESH
F32 = jnp.float32
BF16 = jnp.bfloat16


def pack(rows):
    parts = [rows[:, k : k + 128] for k in range(0, rows.shape[1], 128)]
    return jnp.concatenate(parts, axis=0).astype(BF16)


def unpack(packed, count):
    wide = packed.astype(F32)
    return jnp.concatenate(
        [wide[k : k + count] for k in range(0, wide.shape[0], count)], axis=1
    )


def read(view, rows):
    return jnp.concatenate([view[k, rows, :] for k in range(view.shape[0])], axis=1)


def write(view, rows, value):
    for k in range(view.shape[0]):
        view[k, rows, :] = value[:, 128 * k : 128 * (k + 1)]


def span_diff(tile):
    size = tile.shape[0]
    place = lax.broadcasted_iota(jnp.int32, tile.shape, 0)
    above = jnp.where(place == size - 1, 0.0, pltpu.roll(tile, size - 1, 0))
    below = jnp.where(place == 0, 0.0, pltpu.roll(tile, 1, 0))
    return above - below


def depth_diff(tiles):
    place = lax.broadcasted_iota(jnp.int32, tiles[0].shape, 1)
    ups = [pltpu.roll(tile, 127, 1) for tile in tiles] + [0.0]
    downs = [0.0] + [pltpu.roll(tile, 1, 1) for tile in tiles]
    return [
        jnp.where(place == 127, ups[k + 1], ups[k]) - jnp.where(place == 0, downs[k], downs[k + 1])
        for k in range(len(tiles))
    ]


def kernel(
    dims,
    init_hbm, states_hbm, index_hbm, inverse_hbm, filter_hbm, turbine_hbm, tile_hbm,
    out_hbm, total_ref,
    adj, states, index_s, inverse, filters, turbine_s, tile_s,
    inv_hi, inv_lo, solved, vel, history, pick, weight, terms,
    send_v, recv_v, send_s, recv_s,
    part_y, got_y, part_x, got_x,
    load_sem, out_sem, sv_sem, rv_sem, ss_sem, rs_sem, sy_sem, ry_sem, sx_sem, rx_sem,
):
    ngx, ngy, comps, sx, sy, steps, slots, points, turbines = dims
    cols = sx * sy
    halves = adj.shape[0]
    levels = 128 * halves
    everything = pl.ds(0, comps * cols)
    gx, gy = lax.axis_index("gx"), lax.axis_index("gy")

    loads = [
        pltpu.make_async_copy(src, dst, load_sem.at[k])
        for k, (src, dst) in enumerate((
            (index_hbm, index_s), (states_hbm, states), (inverse_hbm, inverse),
            (turbine_hbm, turbine_s), (tile_hbm, tile_s), (filter_hbm, filters),
            *((init_hbm.at[:, pl.ds(128 * k, 128)], adj.at[k]) for k in range(halves)),
        ))
    ]
    for load in loads:
        load.start()

    barrier = pltpu.get_barrier_semaphore()

    def greet_x(k, c):
        pl.semaphore_signal(barrier, inc=1, device_id=(lax.rem(gx + k, ngx), gy), device_id_type=MESH)
        return c

    def greet_y(k, c):
        pl.semaphore_signal(barrier, inc=1, device_id=(gx, lax.rem(gy + k, ngy)), device_id_type=MESH)
        return c

    lax.fori_loop(1, ngx, greet_x, 0)
    lax.fori_loop(1, ngy, greet_y, 0)

    beside = (
        (lax.rem(gx + ngx - 1, ngx), gy),
        (lax.rem(gx + 1, ngx), gy),
        (gx, lax.rem(gy + ngy - 1, ngy)),
        (gx, lax.rem(gy + 1, ngy)),
    )

    def edge(c, side):
        base = c * cols
        if side == 0:
            return pl.ds(base, sy)
        if side == 1:
            return pl.ds(base + cols - sy, sy)
        return pl.ds(base + (0 if side == 2 else sy - 1), sx, stride=sy)

    def take(view, c, side):
        return read(view, edge(c, side))

    def put(view, c, side, value):
        write(view, edge(c, side), value)

    def stage(view, staging, s, sides):
        for side in sides:
            staging[s, side] = pack(
                jnp.concatenate([take(view, c, side) for c in range(comps)], axis=0)
            )

    def copy(staging, landing, ssem, rsem, s, side):
        return pltpu.make_async_remote_copy(
            src_ref=staging.at[s, side],
            dst_ref=landing.at[s, side ^ 1],
            send_sem=ssem.at[s, side],
            recv_sem=rsem.at[s, side ^ 1],
            device_id=beside[side],
            device_id_type=MESH,
        )

    def copies(*refs):
        return [copy(*refs, side) for side in range(4)]

    def prepare(s):
        write(vel.at[s], everything, states[index_s[s]].astype(F32))
        stage(vel.at[s], send_v, s, range(4))

    def product(value):
        hi = value.astype(BF16)
        lo = (value - hi.astype(F32)).astype(BF16)
        dot = functools.partial(jnp.dot, preferred_element_type=F32)
        return dot(hi, inv_hi[...]) + (dot(hi, inv_lo[...]) + dot(lo, inv_hi[...]))

    def send(staging, landing, ssem, rsem, s, sides):
        for side in sides:
            copy(staging, landing, ssem, rsem, s, side).start()

    def local(s):
        def field(view, c, x):
            if x < 0 or x >= sx:
                return [jnp.zeros((sy, 128), F32)] * halves
            return [view[k, pl.ds(c * cols + x * sy, sy), :] for k in range(halves)]

        def diffs(view, c, x):
            mid = field(view, c, x)
            low, high = field(view, c, x - 1), field(view, c, x + 1)
            return (
                [high[k] - low[k] for k in range(halves)],
                [span_diff(tile) for tile in mid],
                depth_diff(mid),
            )

        speed = vel.at[s]
        for x in range(sx):
            speeds = [field(speed, c, x) for c in range(comps)]
            now = [field(solved, c, x) for c in range(comps)]
            slopes = [diffs(speed, c, x) for c in range(comps)]
            for c in range(comps):
                own = diffs(solved, c, x)
                for k in range(halves):
                    total = speeds[0][k] * own[0][k] - now[0][k] * slopes[0][c][k]
                    for d in range(1, comps):
                        total = total + speeds[d][k] * own[d][k]
                        total = total - now[d][k] * slopes[d][c][k]
                    adj[k, pl.ds(c * cols + x * sy, sy), :] = now[c][k] + HALF * total

    def couple(s, side):
        sign = -HALF if side % 2 == 0 else HALF
        across = side // 2
        width = sy if across == 0 else sx
        far_speed = unpack(recv_v[s, side], comps * width)
        total = take(solved, 0, side) * far_speed[:width]
        for d in range(1, comps):
            total = total + take(solved, d, side) * far_speed[d * width : (d + 1) * width]
        put(adj, across, side, take(adj, across, side) - sign * total)

    def advect(s, side):
        sign = -HALF if side % 2 == 0 else HALF
        across = side // 2
        width = sy if across == 0 else sx
        far = unpack(recv_s[s, side], comps * width)
        carrier = sign * take(vel.at[s], across, side)
        fresh = []
        for c in range(comps):
            new = take(adj, c, side) + carrier * far[c * width : (c + 1) * width]
            put(adj, c, side, new)
            fresh.append(new)
        return fresh

    rows = lax.broadcasted_iota(jnp.int32, (2 * slots, cols), 0)
    places = lax.broadcasted_iota(jnp.int32, (2 * slots, cols), 1)
    lanes = got_x.shape[-1]
    span = slots * points
    slot_row = lax.broadcasted_iota(jnp.int32, (slots, span), 0) * points
    slot_col = lax.broadcasted_iota(jnp.int32, (slots, span), 1)
    inside = (slot_col >= slot_row) & (slot_col < slot_row + points)

    def look(sources):
        vectors = []
        for source in sources:
            found = jnp.dot(pick[...], source, preferred_element_type=F32)
            vectors.append(jnp.concatenate([found[:slots], found[slots:]], axis=1))
        stacked = vectors[0] if len(vectors) == 1 else jnp.concatenate(vectors, axis=0)
        return lax.dot_general(
            stacked.astype(BF16), filters[...], (((1,), (1,)), ((), ())), preferred_element_type=F32
        )

    loads[2].wait()
    whole = inverse[...]
    high = whole.astype(BF16)
    inv_hi[...] = high
    inv_lo[...] = (whole - high.astype(F32)).astype(BF16)
    for load in loads[6:]:
        load.wait()
    write(solved, everything, product(read(adj, everything)))
    stage(solved, send_s, 0, range(4))
    loads[0].wait()
    loads[1].wait()
    prepare(0)

    pl.semaphore_wait(barrier, ngx - 1 + ngy - 1)
    send(send_s, recv_s, ss_sem, rs_sem, 0, range(4))
    send(send_v, recv_v, sv_sem, rv_sem, 0, range(4))

    for load in loads[3:6]:
        load.wait()
    wanted = jnp.zeros((2 * slots, cols), jnp.int32)
    for j in range(slots):
        first = 2 * tile_s[0, 0, j]
        wanted = jnp.where(rows == j, first, wanted)
        wanted = jnp.where(rows == slots + j, first + 1, wanted)
    pick[...] = jnp.where(wanted == places, 1.0, 0.0).astype(BF16)
    history[...] = jnp.zeros_like(history)
    weight[...] = jnp.zeros_like(weight)
    terms[...] = jnp.zeros_like(terms)

    def step(s, carry):
        @pl.when(s < steps - 1)
        def _():
            prepare(s + 1)
            send(send_v, recv_v, sv_sem, rv_sem, s + 1, range(4))

        local(s)
        for side in range(4):
            copy(send_v, recv_v, sv_sem, rv_sem, s, side ^ 1).wait_recv()
            couple(s, side)
        for side in (2, 3):
            copy(send_s, recv_s, ss_sem, rs_sem, s, side ^ 1).wait_recv()
            advect(s, side)

        @pl.when(s < steps - 1)
        def _():
            write(solved, everything, product(read(adj, everything)))

        seen = look((history[...], read(vel.at[s], pl.ds(0, cols)).astype(BF16)))
        terms[...] += weight[...] * seen[:slots]
        speeds = seen[slots:]
        weight[...] = jnp.where(inside, speeds * speeds, 0.0) * (1.0 / points)

        for side in (0, 1):
            copy(send_s, recv_s, ss_sem, rs_sem, s, side ^ 1).wait_recv()
        fresh = advect(s, 0) + advect(s, 1)

        @pl.when(s < steps - 1)
        def _():
            edges = product(jnp.concatenate(fresh, axis=0))
            for side in (0, 1):
                part = edges[side * comps * sy : (side + 1) * comps * sy]
                send_s[s + 1, side] = pack(part)
                send(send_s, recv_s, ss_sem, rs_sem, s + 1, (side,))
                for c in range(comps):
                    put(solved, c, side, part[c * sy : (c + 1) * sy])
            stage(solved, send_s, s + 1, (2, 3))
            send(send_s, recv_s, ss_sem, rs_sem, s + 1, (2, 3))

        history[...] = read(adj, pl.ds(0, cols)).astype(BF16)
        return carry

    lax.fori_loop(0, steps, step, 0)

    outs = [
        pltpu.make_async_copy(adj.at[k], out_hbm.at[:, pl.ds(128 * k, 128)], out_sem.at[k])
        for k in range(halves)
    ]
    for out in outs:
        out.start()

    term = jnp.sum(terms[...] + weight[...] * look((history[...],)), axis=1, keepdims=True)
    slot_rows = lax.broadcasted_iota(jnp.int32, (slots, lanes), 0)
    lane = lax.broadcasted_iota(jnp.int32, (slots, lanes), 1)
    named = jnp.full((slots, lanes), turbines, jnp.int32)
    for j in range(slots):
        named = jnp.where(slot_rows == j, turbine_s[0, 0, j], named)
    live = (named == lane) & (lane < turbines)
    part_y[...] = jnp.sum(jnp.where(live, term, 0.0), axis=0, keepdims=True)

    def span_copy(k):
        return pltpu.make_async_remote_copy(
            src_ref=part_y, dst_ref=got_y.at[k - 1],
            send_sem=sy_sem.at[k - 1], recv_sem=ry_sem.at[k - 1],
            device_id=(gx, lax.rem(gy + k, ngy)), device_id_type=MESH,
        )

    def stream_copy(k):
        return pltpu.make_async_remote_copy(
            src_ref=part_x, dst_ref=got_x.at[k - 1],
            send_sem=sx_sem.at[k - 1], recv_sem=rx_sem.at[k - 1],
            device_id=(lax.rem(gx + k, ngx), gy), device_id_type=MESH,
        )

    def run(make, count, act):
        def one(k, c):
            act(make(k))
            return c
        lax.fori_loop(1, count, one, 0)

    run(span_copy, ngy, lambda c: c.start())
    run(span_copy, ngy, lambda c: c.wait_recv())
    part_x[...] = part_y[...] + jnp.sum(got_y[...], axis=0)
    run(stream_copy, ngx, lambda c: c.start())
    run(stream_copy, ngx, lambda c: c.wait_recv())
    summed = part_x[...] + jnp.sum(got_x[...], axis=0)
    total_ref[...] = summed[:, :turbines].reshape(total_ref.shape)

    def drain(s, c):
        for sent in copies(send_v, recv_v, sv_sem, rv_sem, s):
            sent.wait_send()
        for sent in copies(send_s, recv_s, ss_sem, rs_sem, s):
            sent.wait_send()
        return c

    lax.fori_loop(0, steps, drain, 0)
    run(span_copy, ngy, lambda c: c.wait_send())
    run(stream_copy, ngx, lambda c: c.wait_send())
    for out in outs:
        out.wait()


def body(sizes, adjoint_init, saved_states, step_index, vertical_inverse, disk_filter,
         pair_turbine, pair_tile, turbine_owner):
    ngx, ngy = sizes
    comps, sx, sy, levels = adjoint_init.shape
    saved = saved_states.shape[0]
    steps = step_index.shape[0]
    slots, points, cells = disk_filter.shape[2:]
    turbines = turbine_owner.shape[0]
    rows = comps * sx * sy
    lanes = -(-turbines // 128) * 128
    packed = comps * max(sx, sy) * levels // 128
    halves = levels // 128
    dims = (ngx, ngy, comps, sx, sy, steps, slots, points, turbines)
    anywhere = pl.BlockSpec(memory_space=pl.ANY)
    halo = pltpu.VMEM((steps, 4, packed, 128), BF16)
    dma = pltpu.SemaphoreType.DMA
    final, totals = pl.pallas_call(
        functools.partial(kernel, dims),
        out_shape=(
            jax.ShapeDtypeStruct((rows, levels), F32),
            jax.ShapeDtypeStruct((1, 1, turbines), F32),
        ),
        in_specs=[pl.BlockSpec(memory_space=pltpu.HBM)] * 7,
        out_specs=(anywhere, pl.BlockSpec(memory_space=pltpu.VMEM)),
        scratch_shapes=[
            pltpu.VMEM((halves, rows, 128), F32),
            pltpu.VMEM((saved, rows, levels), BF16),
            pltpu.SMEM(step_index.shape, jnp.int32),
            pltpu.VMEM((levels, levels), F32),
            pltpu.VMEM((slots * points, cells), BF16),
            pltpu.SMEM(pair_turbine.shape, jnp.int32),
            pltpu.SMEM(pair_tile.shape, jnp.int32),
            pltpu.VMEM((levels, levels), BF16),
            pltpu.VMEM((levels, levels), BF16),
            pltpu.VMEM((halves, rows, 128), F32),
            pltpu.VMEM((steps, halves, rows, 128), F32),
            pltpu.VMEM((sx * sy, levels), BF16),
            pltpu.VMEM((2 * slots, sx * sy), BF16),
            pltpu.VMEM((slots, slots * points), F32),
            pltpu.VMEM((slots, slots * points), F32),
            halo, halo, halo, halo,
            pltpu.VMEM((1, lanes), F32),
            pltpu.VMEM((ngy - 1, 1, lanes), F32),
            pltpu.VMEM((1, lanes), F32),
            pltpu.VMEM((ngx - 1, 1, lanes), F32),
            dma((6 + halves,)), dma((halves,)),
            dma((steps, 4)), dma((steps, 4)), dma((steps, 4)), dma((steps, 4)),
            dma((ngy - 1,)), dma((ngy - 1,)), dma((ngx - 1,)), dma((ngx - 1,)),
        ],
        compiler_params=pltpu.CompilerParams(
            collective_id=0, has_side_effects=True, vmem_limit_bytes=60 * 1024 * 1024
        ),
        name="sweep",
    )(
        adjoint_init.reshape(rows, levels),
        saved_states.reshape(saved, rows, levels),
        step_index,
        vertical_inverse,
        disk_filter.reshape(slots * points, cells),
        pair_turbine,
        pair_tile,
    )
    own = lax.axis_index("gx") * ngy + lax.axis_index("gy")
    grad = jnp.where(turbine_owner[None, None, :] == own, totals, 0.0)
    return final.reshape(adjoint_init.shape), grad


def solution(mesh):
    placed = (
        P(None, "gx", "gy", None),
        P(None, None, "gx", "gy", None),
        P(),
        P(),
        P("gx", "gy", None, None, None),
        P("gx", "gy", None),
        P("gx", "gy", None),
        P(),
    )
    return jax.shard_map(
        functools.partial(body, (mesh.shape["gx"], mesh.shape["gy"])),
        mesh=mesh,
        in_specs=placed,
        out_specs=(P(None, "gx", "gy", None), P("gx", "gy", None)),
        check_vma=False,
    )
```

time: 37 us -> 35.1 us (0.949)
  local copies, waits for them, and re-layouts: 5.77 us -> 2.26 us
  Pallas kernels: 30.3 us -> 31.4 us
  other arithmetic: 0 us -> 0.51 us
    unnamed x18 -> x5, local copies, waits for them, and re-layouts: 5.77 us -> 2.26 us
    pallas_call x1, Pallas kernels: 30.3 us -> 31.4 us  [body(): pl.pallas_call(functools.partial(kernel, dims), out_shape=(jax.ShapeDtype...]
    select_n x0 -> x1, other arithmetic: none -> 0.51 us  [body(): grad = jnp.where(turbine_owner[None, None, :] == own, totals, 0.0)]
where the time goes in v2:
time: 35.1 us; the launch traced here: 34.9 us
  Pallas kernels  31.4 us (89%)
  local copies, waits for them, and re-layouts  2.26 us (6%)
  between operations  0.66 us (2%)
  other arithmetic  0.51 us (1%)
    pallas_call x1, Pallas kernels, body(): pl.pallas_call(functools.partial(kernel, dims), out_shape=(jax.ShapeDtype...  31.4 us
    unnamed x5, local copies, waits for them, and re-layouts  2.26 us

profile of v2, /device:TPU:0, one launch (start us, length us, event | category | flops | bytes accessed | tf_op | source)
XLA Modules:
  0.0 34.9 jit_solution(2785724256010226395)
XLA Ops:
  0.6 31.4 %sweep.1 = (f32[192,256]{1,0:T(8,128)}, f32[1,1,24]{2,1,0:T(1,128)}) custom-call(f32[192,256]{1,0:T(8,128)} %bitcast.9, bf16[4,192,256]{2,1,0:T(8,128)(2,1)} %bitcast.7, s32[4]{0:T(128)} %index_hbm.1, f32[256,256]{1,0:T(8,128)} %inverse_hbm.1, bf16[512,512]{1,0:T(8,128)(2,1)} %bitcast.6, s32[1,1,8]{2,1,0:T(1,128)} %turbine_hbm.1, s32[1,1,8]{2,1,0:T(1,128)} %tile_hbm.1), custom_call_target="tpu_custom_call" | custom-call | tf_op jit(solution)/shard_map/sweep/pallas_call | solution.py:368
  32.1 0.0 copy-start
  32.1 0.0 copy-start.1
  32.1 0.6 %copy-done = s32[24]{0:T(128)S(1)} copy-done((s32[24]{0:T(128)S(1)}, s32[24]{0:T(128)}, u32[]{:S(2)}) %copy-start) | copy-done | bytes 120
  32.7 0.0 copy-done.1
  32.8 0.5 %bitcast_select_fusion = f32[1,1,24]{2,1,0:T(1,128)} fusion(f32[1,1,24]{2,1,0:T(1,128)S(1)} %copy-done.1, s32[24]{0:T(128)S(1)} %copy-done, s32[]{:T(128)S(6)} %add.3), kind=kLoop, calls=%fused_computation | loop fusion | flops 48 | bytes 292 | tf_op jit(solution)/shard_map/jit(_where)/select_n | solution.py:415
  33.3 1.6 %copy.11 = f32[3,8,8,256]{3,2,1,0:T(8,128)} copy(f32[3,8,8,256]{3,2,1,0:T(8,128)} %bitcast.8) | data formatting | bytes 393216
Async XLA Ops:
  32.1 0.7 %copy-start = (s32[24]{0:T(128)S(1)}, s32[24]{0:T(128)}, u32[]{:S(2)}) copy-start(s32[24]{0:T(128)} %param.15) | copy-start | bytes 292
  32.1 0.6 %copy-start.1 = (f32[1,1,24]{2,1,0:T(1,128)S(1)}, f32[1,1,24]{2,1,0:T(1,128)}, u32[]{:S(2)}) copy-start(f32[1,1,24]{2,1,0:T(1,128)} %get-tuple-element.5) | copy-start | bytes 292

commit v3 on v2

v3 whole, which is shorter than its diff:
```python
import functools

import jax
import jax.numpy as jnp
from jax import lax
from jax.experimental import pallas as pl
from jax.experimental.pallas import tpu as pltpu
from jax.sharding import PartitionSpec as P

COURANT = 0.2
HALF = 0.5 * COURANT
MESH = pl.DeviceIdType.MESH
F32 = jnp.float32
BF16 = jnp.bfloat16


def pack(rows):
    parts = [rows[:, k : k + 128] for k in range(0, rows.shape[1], 128)]
    return jnp.concatenate(parts, axis=0).astype(BF16)


def unpack(packed, count):
    wide = packed.astype(F32)
    return jnp.concatenate(
        [wide[k : k + count] for k in range(0, wide.shape[0], count)], axis=1
    )


def read(view, rows):
    return jnp.concatenate([view[k, rows, :] for k in range(view.shape[0])], axis=1)


def write(view, rows, value):
    for k in range(view.shape[0]):
        view[k, rows, :] = value[:, 128 * k : 128 * (k + 1)]


def row_diff(tile, low=0.0, high=0.0):
    size = tile.shape[0]
    place = lax.broadcasted_iota(jnp.int32, tile.shape, 0)
    above = jnp.where(place == size - 1, high, pltpu.roll(tile, size - 1, 0))
    below = jnp.where(place == 0, low, pltpu.roll(tile, 1, 0))
    return above - below


def split(wide):
    return [wide[:, k : k + 128] for k in range(0, wide.shape[1], 128)]


def depth_diff(tiles):
    place = lax.broadcasted_iota(jnp.int32, tiles[0].shape, 1)
    ups = [pltpu.roll(tile, 127, 1) for tile in tiles] + [0.0]
    downs = [0.0] + [pltpu.roll(tile, 1, 1) for tile in tiles]
    return [
        jnp.where(place == 127, ups[k + 1], ups[k]) - jnp.where(place == 0, downs[k], downs[k + 1])
        for k in range(len(tiles))
    ]


def kernel(
    dims,
    init_hbm, states_hbm, index_hbm, inverse_hbm, filter_hbm, turbine_hbm, tile_hbm,
    out_hbm, total_ref,
    adj, states, index_s, inverse, filters, turbine_s, tile_s,
    inv_hi, inv_lo, solved, vel, history, pick, weight, terms,
    send_v, recv_v, send_s, recv_s, send_c, recv_c,
    part, got,
    load_sem, out_sem, sv_sem, rv_sem, ss_sem, rs_sem, sc_sem, rc_sem, st_sem, rt_sem,
):
    ngx, ngy, comps, sx, sy, steps, slots, points, turbines = dims
    cols = sx * sy
    halves = adj.shape[0]
    levels = 128 * halves
    everything = pl.ds(0, comps * cols)
    gx, gy = lax.axis_index("gx"), lax.axis_index("gy")

    loads = [
        pltpu.make_async_copy(src, dst, load_sem.at[k])
        for k, (src, dst) in enumerate((
            (index_hbm, index_s), (states_hbm, states), (inverse_hbm, inverse),
            (turbine_hbm, turbine_s), (tile_hbm, tile_s), (filter_hbm, filters),
            *((init_hbm.at[:, pl.ds(128 * k, 128)], adj.at[k]) for k in range(halves)),
        ))
    ]
    for load in loads:
        load.start()

    barrier = pltpu.get_barrier_semaphore()

    count = ngx * ngy
    me = gx * ngy + gy

    def peer(k):
        other = lax.rem(me + k, count)
        return (other // ngy, lax.rem(other, ngy))

    def greet(k, c):
        pl.semaphore_signal(barrier, inc=1, device_id=peer(k), device_id_type=MESH)
        return c

    lax.fori_loop(1, count, greet, 0)

    beside_x = (lax.rem(gx + ngx - 1, ngx), lax.rem(gx + 1, ngx))
    beside_y = (lax.rem(gy + ngy - 1, ngy), lax.rem(gy + 1, ngy))
    beside = [(x, gy) for x in beside_x] + [(gx, y) for y in beside_y]
    aslant = [(x, y) for x in beside_x for y in beside_y]

    def edge(c, side, depth):
        base = c * cols
        if side == 0:
            return pl.ds(base + depth * sy, sy)
        if side == 1:
            return pl.ds(base + cols - (depth + 1) * sy, sy)
        return pl.ds(base + (depth if side == 2 else sy - 1 - depth), sx, stride=sy)

    def take(view, c, side, depth=0):
        return read(view, edge(c, side, depth))

    def put(view, c, side, value):
        write(view, edge(c, side, 0), value)

    def strips(view, side, depths):
        return [take(view, c, side, depth) for depth in depths for c in range(comps)]

    def stage_speed(r):
        for s in (2 * r, 2 * r + 1):
            write(vel.at[s], everything, states[index_s[s]].astype(F32))
        for side in range(4):
            parts = strips(vel.at[2 * r], side, (0, 1)) + strips(vel.at[2 * r + 1], side, (0,))
            send_v[r, side] = pack(jnp.concatenate(parts, axis=0))

    def stage_solved(r):
        for side in range(4):
            send_s[r, side] = pack(jnp.concatenate(strips(solved, side, (0, 1)), axis=0))
        place = lax.broadcasted_iota(jnp.int32, (8, 128), 0)
        for q in range(4):
            cell = (q // 2) * (sx - 1) * sy + (q % 2) * (sy - 1)
            tiles = []
            for k in range(halves):
                tile = jnp.zeros((8, 128), F32)
                for c in range(comps):
                    row = pl.ds(c * cols + cell, 1)
                    tile = jnp.where(place == c, solved[k, row, :], tile)
                    tile = jnp.where(place == comps + c, vel[2 * r, k, row, :], tile)
                tiles.append(tile)
            send_c[r, q] = jnp.concatenate(tiles, axis=0).astype(BF16)

    def remote(staging, landing, ssem, rsem, r, k, flip, where):
        return pltpu.make_async_remote_copy(
            src_ref=staging.at[r, k],
            dst_ref=landing.at[r, k ^ flip],
            send_sem=ssem.at[r, k],
            recv_sem=rsem.at[r, k ^ flip],
            device_id=where[k],
            device_id_type=MESH,
        )

    def speed_copy(r, side):
        return remote(send_v, recv_v, sv_sem, rv_sem, r, side, 1, beside)

    def solved_copy(r, side):
        return remote(send_s, recv_s, ss_sem, rs_sem, r, side, 1, beside)

    def corner_copy(r, q):
        return remote(send_c, recv_c, sc_sem, rc_sem, r, q, 3, aslant)

    def split_corner(packed):
        wide = packed.astype(F32)
        return [wide[8 * k : 8 * (k + 1)] for k in range(halves)]

    def product(value):
        hi = value.astype(BF16)
        lo = (value - hi.astype(F32)).astype(BF16)
        dot = functools.partial(jnp.dot, preferred_element_type=F32)
        return dot(hi, inv_hi[...]) + (dot(hi, inv_lo[...]) + dot(lo, inv_hi[...]))

    def local(s):
        def field(view, c, x):
            if x < 0 or x >= sx:
                return [jnp.zeros((sy, 128), F32)] * halves
            return [view[k, pl.ds(c * cols + x * sy, sy), :] for k in range(halves)]

        def diffs(view, c, x):
            mid = field(view, c, x)
            low, high = field(view, c, x - 1), field(view, c, x + 1)
            return (
                [high[k] - low[k] for k in range(halves)],
                [row_diff(tile) for tile in mid],
                depth_diff(mid),
            )

        speed = vel.at[s]
        for x in range(sx):
            speeds = [field(speed, c, x) for c in range(comps)]
            now = [field(solved, c, x) for c in range(comps)]
            slopes = [diffs(speed, c, x) for c in range(comps)]
            for c in range(comps):
                own = diffs(solved, c, x)
                for k in range(halves):
                    total = speeds[0][k] * own[0][k] - now[0][k] * slopes[0][c][k]
                    for d in range(1, comps):
                        total = total + speeds[d][k] * own[d][k]
                        total = total - now[d][k] * slopes[d][c][k]
                    adj[k, pl.ds(c * cols + x * sy, sy), :] = now[c][k] + HALF * total

    def triples(packed, side):
        width = sy if side < 2 else sx
        wide = unpack(packed, packed.shape[0] // halves)
        return [
            [split(wide[i + c * width : i + (c + 1) * width]) for c in range(comps)]
            for i in range(0, wide.shape[0], comps * width)
        ]

    def fix(s, side, far, far_speed):
        sign = -HALF if side % 2 == 0 else HALF
        across = side // 2
        rows = edge(0, side, 0)
        for k in range(halves):
            at = lambda view, c: view[k, edge(c, side, 0), :]
            carrier = sign * at(vel.at[s], across)
            for c in range(comps):
                new = at(adj, c) + carrier * far[c][k]
                if c == across:
                    total = at(solved, 0) * far_speed[0][k]
                    for d in range(1, comps):
                        total = total + at(solved, d) * far_speed[d][k]
                    new = new - sign * total
                adj[k, edge(c, side, 0), :] = new

    def outside(r, side, far, far_speed, corners):
        across, along = side // 2, 1 - side // 2
        ends = (2 * (side % 2), 2 * (side % 2) + 1) if across == 0 else (side % 2, 2 + side % 2)

        def normal(inner, outer):
            return [(i - o) if side % 2 == 0 else (o - i) for i, o in zip(inner, outer)]

        def diffs(c, view, strip, base):
            mid, outer = strip[0][c], strip[1][c]
            slopes = [None] * 3
            slopes[across] = normal(split(take(view, c, side)), outer)
            row = base + c
            slopes[along] = [
                row_diff(
                    mid[k],
                    corners[ends[0]][k][row : row + 1],
                    corners[ends[1]][k][row : row + 1],
                )
                for k in range(halves)
            ]
            slopes[2] = depth_diff(mid)
            return slopes

        own = [diffs(c, solved, far, 0) for c in range(comps)]
        speed = [diffs(c, vel.at[2 * r], far_speed, comps) for c in range(comps)]
        news = []
        for c in range(comps):
            tiles = []
            for k in range(halves):
                total = far_speed[0][0][k] * own[c][0][k] - far[0][0][k] * speed[0][c][k]
                for d in range(1, comps):
                    total = total + far_speed[0][d][k] * own[c][d][k]
                    total = total - far[0][d][k] * speed[d][c][k]
                tiles.append(far[0][c][k] + HALF * total)
            news.append(jnp.concatenate(tiles, axis=1))
        return news

    rows = lax.broadcasted_iota(jnp.int32, (2 * slots, cols), 0)
    places = lax.broadcasted_iota(jnp.int32, (2 * slots, cols), 1)
    lanes = got.shape[-1]
    span = slots * points
    slot_row = lax.broadcasted_iota(jnp.int32, (slots, span), 0) * points
    slot_col = lax.broadcasted_iota(jnp.int32, (slots, span), 1)
    inside = (slot_col >= slot_row) & (slot_col < slot_row + points)

    def look(sources):
        vectors = []
        for source in sources:
            found = jnp.dot(pick[...], source, preferred_element_type=F32)
            vectors.append(jnp.concatenate([found[:slots], found[slots:]], axis=1))
        stacked = vectors[0] if len(vectors) == 1 else jnp.concatenate(vectors, axis=0)
        return lax.dot_general(
            stacked.astype(BF16), filters[...], (((1,), (1,)), ((), ())), preferred_element_type=F32
        )

    loads[2].wait()
    whole = inverse[...]
    high = whole.astype(BF16)
    inv_hi[...] = high
    inv_lo[...] = (whole - high.astype(F32)).astype(BF16)
    for load in loads[6:]:
        load.wait()
    write(solved, everything, product(read(adj, everything)))
    loads[0].wait()
    loads[1].wait()
    stage_speed(0)
    stage_solved(0)

    pl.semaphore_wait(barrier, count - 1)
    for k in range(4):
        solved_copy(0, k).start()
        corner_copy(0, k).start()
        speed_copy(0, k).start()

    for load in loads[3:6]:
        load.wait()
    wanted = jnp.zeros((2 * slots, cols), jnp.int32)
    for j in range(slots):
        first = 2 * tile_s[0, 0, j]
        wanted = jnp.where(rows == j, first, wanted)
        wanted = jnp.where(rows == slots + j, first + 1, wanted)
    pick[...] = jnp.where(wanted == places, 1.0, 0.0).astype(BF16)
    history[...] = jnp.zeros_like(history)
    weight[...] = jnp.zeros_like(weight)
    terms[...] = jnp.zeros_like(terms)

    def pair(r, carry):
        first, second = 2 * r, 2 * r + 1

        @pl.when(r < steps // 2 - 1)
        def _():
            stage_speed(r + 1)
            for side in range(4):
                speed_copy(r + 1, side).start()

        local(first)
        sources = [history[i] for i in range(2)]
        sources += [read(vel.at[s], pl.ds(0, cols)).astype(BF16) for s in (first, second)]
        seen = look(sources)
        parts = [seen[i * slots : (i + 1) * slots] for i in range(4)]
        terms[...] += weight[0] * parts[0] + weight[1] * parts[1]
        for i in range(2):
            weight[i] = jnp.where(inside, parts[2 + i] * parts[2 + i], 0.0) * (1.0 / points)

        for k in range(4):
            speed_copy(r, k ^ 1).wait_recv()
            corner_copy(r, k ^ 3).wait_recv()
            solved_copy(r, k ^ 1).wait_recv()
        corners = [split_corner(recv_c[r, q]) for q in range(4)]
        ring = []
        for side in range(4):
            far = triples(recv_s[r, side], side)
            far_speed = triples(recv_v[r, side], side)
            fix(first, side, far[0], far_speed[0])
            ring += outside(r, side, far, far_speed, corners)
        history[0] = read(adj, pl.ds(0, cols)).astype(BF16)
        outer = product(jnp.concatenate(ring, axis=0))
        write(solved, everything, product(read(adj, everything)))

        local(second)
        start = 0
        for side in range(4):
            width = sy if side < 2 else sx
            far = [split(outer[start + c * width : start + (c + 1) * width]) for c in range(comps)]
            start += comps * width
            fix(second, side, far, triples(recv_v[r, side], side)[2])
        history[1] = read(adj, pl.ds(0, cols)).astype(BF16)

        @pl.when(r < steps // 2 - 1)
        def _():
            write(solved, everything, product(read(adj, everything)))
            stage_solved(r + 1)
            for k in range(4):
                solved_copy(r + 1, k).start()
                corner_copy(r + 1, k).start()

        return carry

    lax.fori_loop(0, steps // 2, pair, 0)

    outs = [
        pltpu.make_async_copy(adj.at[k], out_hbm.at[:, pl.ds(128 * k, 128)], out_sem.at[k])
        for k in range(halves)
    ]
    for out in outs:
        out.start()

    seen = look([history[i] for i in range(2)])
    total = terms[...] + weight[0] * seen[:slots] + weight[1] * seen[slots:]
    term = jnp.sum(total, axis=1, keepdims=True)
    slot_rows = lax.broadcasted_iota(jnp.int32, (slots, lanes), 0)
    lane = lax.broadcasted_iota(jnp.int32, (slots, lanes), 1)
    named = jnp.full((slots, lanes), turbines, jnp.int32)
    for j in range(slots):
        named = jnp.where(slot_rows == j, turbine_s[0, 0, j], named)
    live = (named == lane) & (lane < turbines)
    part[...] = jnp.sum(jnp.where(live, term, 0.0), axis=0, keepdims=True)

    def share(k):
        return pltpu.make_async_remote_copy(
            src_ref=part, dst_ref=got.at[k - 1],
            send_sem=st_sem.at[k - 1], recv_sem=rt_sem.at[k - 1],
            device_id=peer(k), device_id_type=MESH,
        )

    def run(act):
        def one(k, c):
            act(share(k))
            return c
        lax.fori_loop(1, count, one, 0)

    run(lambda c: c.start())

    def drain(r, c):
        for k in range(4):
            speed_copy(r, k).wait_send()
            solved_copy(r, k).wait_send()
            corner_copy(r, k).wait_send()
        return c

    lax.fori_loop(0, steps // 2, drain, 0)
    run(lambda c: c.wait_recv())
    summed = part[...] + jnp.sum(got[...], axis=0)
    total_ref[...] = summed[:, :turbines].reshape(total_ref.shape)
    run(lambda c: c.wait_send())
    for out in outs:
        out.wait()


def body(sizes, adjoint_init, saved_states, step_index, vertical_inverse, disk_filter,
         pair_turbine, pair_tile, turbine_owner):
    ngx, ngy = sizes
    comps, sx, sy, levels = adjoint_init.shape
    saved = saved_states.shape[0]
    steps = step_index.shape[0]
    slots, points, cells = disk_filter.shape[2:]
    turbines = turbine_owner.shape[0]
    rows = comps * sx * sy
    lanes = -(-turbines // 128) * 128
    strip = comps * max(sx, sy) * levels // 128
    halves = levels // 128
    rounds = steps // 2
    count = ngx * ngy
    assert steps % 2 == 0 and sx == sy
    dims = (ngx, ngy, comps, sx, sy, steps, slots, points, turbines)
    anywhere = pl.BlockSpec(memory_space=pl.ANY)
    halo = lambda rows: pltpu.VMEM((rounds, 4, rows, 128), BF16)
    dma = pltpu.SemaphoreType.DMA
    final, totals = pl.pallas_call(
        functools.partial(kernel, dims),
        out_shape=(
            jax.ShapeDtypeStruct((rows, levels), F32),
            jax.ShapeDtypeStruct((1, 1, turbines), F32),
        ),
        in_specs=[pl.BlockSpec(memory_space=pltpu.HBM)] * 7,
        out_specs=(anywhere, pl.BlockSpec(memory_space=pltpu.VMEM)),
        scratch_shapes=[
            pltpu.VMEM((halves, rows, 128), F32),
            pltpu.VMEM((saved, rows, levels), BF16),
            pltpu.SMEM(step_index.shape, jnp.int32),
            pltpu.VMEM((levels, levels), F32),
            pltpu.VMEM((slots * points, cells), BF16),
            pltpu.SMEM(pair_turbine.shape, jnp.int32),
            pltpu.SMEM(pair_tile.shape, jnp.int32),
            pltpu.VMEM((levels, levels), BF16),
            pltpu.VMEM((levels, levels), BF16),
            pltpu.VMEM((halves, rows, 128), F32),
            pltpu.VMEM((steps, halves, rows, 128), F32),
            pltpu.VMEM((2, sx * sy, levels), BF16),
            pltpu.VMEM((2 * slots, sx * sy), BF16),
            pltpu.VMEM((2, slots, slots * points), F32),
            pltpu.VMEM((slots, slots * points), F32),
            halo(3 * strip), halo(3 * strip), halo(2 * strip), halo(2 * strip),
            halo(8 * halves), halo(8 * halves),
            pltpu.VMEM((1, lanes), F32),
            pltpu.VMEM((count - 1, 1, lanes), F32),
            dma((6 + halves,)), dma((halves,)),
            *[dma((rounds, 4))] * 6,
            dma((count - 1,)), dma((count - 1,)),
        ],
        compiler_params=pltpu.CompilerParams(
            collective_id=0, has_side_effects=True, vmem_limit_bytes=60 * 1024 * 1024
        ),
        name="sweep",
    )(
        adjoint_init.reshape(rows, levels),
        saved_states.reshape(saved, rows, levels),
        step_index,
        vertical_inverse,
        disk_filter.reshape(slots * points, cells),
        pair_turbine,
        pair_tile,
    )
    own = lax.axis_index("gx") * ngy + lax.axis_index("gy")
    grad = jnp.where(turbine_owner[None, None, :] == own, totals, 0.0)
    return final.reshape(adjoint_init.shape), grad


def solution(mesh):
    placed = (
        P(None, "gx", "gy", None),
        P(None, None, "gx", "gy", None),
        P(),
        P(),
        P("gx", "gy", None, None, None),
        P("gx", "gy", None),
        P("gx", "gy", None),
        P(),
    )
    return jax.shard_map(
        functools.partial(body, (mesh.shape["gx"], mesh.shape["gy"])),
        mesh=mesh,
        in_specs=placed,
        out_specs=(P(None, "gx", "gy", None), P("gx", "gy", None)),
        check_vma=False,
    )
```

time: 35.1 us -> 27.6 us (0.79)
  Pallas kernels: 31.4 us -> 24 us
    pallas_call x1, Pallas kernels: 31.4 us -> 24 us  [body(): pl.pallas_call(functools.partial(kernel, dims), out_shape=(jax.ShapeDtype...]
where the time goes in v3:
time: 27.6 us; the launch traced here: 27.4 us
  Pallas kernels  24 us (87%)
  local copies, waits for them, and re-layouts  2.26 us (8%)
  between operations  0.66 us (2%)
  other arithmetic  0.51 us (2%)
    pallas_call x1, Pallas kernels, body(): pl.pallas_call(functools.partial(kernel, dims), out_shape=(jax.ShapeDtype...  24 us
    unnamed x5, local copies, waits for them, and re-layouts  2.26 us

profile of v3, /device:TPU:0, one launch (start us, length us, event | category | flops | bytes accessed | tf_op | source)
XLA Modules:
  0.0 27.4 jit_solution(569498738512018148)
XLA Ops:
  0.6 24.0 %sweep.1 = (f32[192,256]{1,0:T(8,128)}, f32[1,1,24]{2,1,0:T(1,128)}) custom-call(f32[192,256]{1,0:T(8,128)} %bitcast.9, bf16[4,192,256]{2,1,0:T(8,128)(2,1)} %bitcast.7, s32[4]{0:T(128)} %index_hbm.1, f32[256,256]{1,0:T(8,128)} %inverse_hbm.1, bf16[512,512]{1,0:T(8,128)(2,1)} %bitcast.6, s32[1,1,8]{2,1,0:T(1,128)} %turbine_hbm.1, s32[1,1,8]{2,1,0:T(1,128)} %tile_hbm.1), custom_call_target="tpu_custom_call" | custom-call | tf_op jit(solution)/shard_map/sweep/pallas_call | solution.py:438
  24.6 0.0 copy-start
  24.7 0.0 copy-start.1
  24.7 0.6 %copy-done = s32[24]{0:T(128)S(1)} copy-done((s32[24]{0:T(128)S(1)}, s32[24]{0:T(128)}, u32[]{:S(2)}) %copy-start) | copy-done | bytes 120
  25.3 0.0 copy-done.1
  25.3 0.5 %bitcast_select_fusion = f32[1,1,24]{2,1,0:T(1,128)} fusion(f32[1,1,24]{2,1,0:T(1,128)S(1)} %copy-done.1, s32[24]{0:T(128)S(1)} %copy-done, s32[]{:T(128)S(6)} %add.3), kind=kLoop, calls=%fused_computation | loop fusion | flops 48 | bytes 292 | tf_op jit(solution)/shard_map/jit(_where)/select_n | solution.py:484
  25.8 1.6 %copy.11 = f32[3,8,8,256]{3,2,1,0:T(8,128)} copy(f32[3,8,8,256]{3,2,1,0:T(8,128)} %bitcast.8) | data formatting | bytes 393216
Async XLA Ops:
  24.6 0.7 %copy-start = (s32[24]{0:T(128)S(1)}, s32[24]{0:T(128)}, u32[]{:S(2)}) copy-start(s32[24]{0:T(128)} %param.15) | copy-start | bytes 292
  24.7 0.6 %copy-start.1 = (f32[1,1,24]{2,1,0:T(1,128)S(1)}, f32[1,1,24]{2,1,0:T(1,128)}, u32[]{:S(2)}) copy-start(f32[1,1,24]{2,1,0:T(1,128)} %get-tuple-element.5) | copy-start | bytes 292

commit v4 on v3

--- a/solution.py
+++ b/solution.py
@@ -59,13 +59,13 @@
 
 def kernel(
     dims,
-    init_hbm, states_hbm, index_hbm, inverse_hbm, filter_hbm, turbine_hbm, tile_hbm,
-    out_hbm, total_ref,
-    adj, states, index_s, inverse, filters, turbine_s, tile_s,
-    inv_hi, inv_lo, solved, vel, history, pick, weight, terms,
-    send_v, recv_v, send_s, recv_s, send_c, recv_c,
+    init_hbm, states_hbm, index_hbm, inverse_hbm, filter_hbm, turbine_hbm, tile_hbm, owner_hbm,
+    out_hbm, grad_hbm,
+    adj, states, index_s, inverse, filters, turbine_s, tile_s, owner_s,
+    inv_hi, inv_lo, solved, vel, history, pick, live, mine, weight, terms, grad,
+    send_v, recv_v, send_w, recv_w, send_s, recv_s, send_c, recv_c,
     part, got,
-    load_sem, out_sem, sv_sem, rv_sem, ss_sem, rs_sem, sc_sem, rc_sem, st_sem, rt_sem,
+    load_sem, out_sem, sv_sem, rv_sem, sw_sem, rw_sem, ss_sem, rs_sem, sc_sem, rc_sem, st_sem, rt_sem,
 ):
     ngx, ngy, comps, sx, sy, steps, slots, points, turbines = dims
     cols = sx * sy
@@ -77,9 +77,9 @@
     loads = [
         pltpu.make_async_copy(src, dst, load_sem.at[k])
         for k, (src, dst) in enumerate((
-            (index_hbm, index_s), (states_hbm, states), (inverse_hbm, inverse),
-            (turbine_hbm, turbine_s), (tile_hbm, tile_s), (filter_hbm, filters),
             *((init_hbm.at[:, pl.ds(128 * k, 128)], adj.at[k]) for k in range(halves)),
+            (inverse_hbm, inverse), (index_hbm, index_s), (states_hbm, states),
+            (turbine_hbm, turbine_s), (tile_hbm, tile_s), (owner_hbm, owner_s), (filter_hbm, filters),
         ))
     ]
     for load in loads:
@@ -91,14 +91,22 @@
     me = gx * ngy + gy
 
     def peer(k):
-        other = lax.rem(me + k, count)
-        return (other // ngy, lax.rem(other, ngy))
-
-    def greet(k, c):
-        pl.semaphore_signal(barrier, inc=1, device_id=peer(k), device_id_type=MESH)
-        return c
-
-    lax.fori_loop(1, count, greet, 0)
+        if isinstance(k, int):
+            x, y = gx + k // ngy, gy + k % ngy
+            return (jnp.where(x >= ngx, x - ngx, x), jnp.where(y >= ngy, y - ngy, y))
+        return (lax.rem(gx + k // ngy, ngx), lax.rem(gy + lax.rem(k, ngy), ngy))
+
+    def others(act):
+        if count <= 64:
+            for k in range(1, count):
+                act(k)
+        else:
+            def one(k, c):
+                act(k)
+                return c
+            lax.fori_loop(1, count, one, 0)
+
+    others(lambda k: pl.semaphore_signal(barrier, inc=1, device_id=peer(k), device_id_type=MESH))
 
     beside_x = (lax.rem(gx + ngx - 1, ngx), lax.rem(gx + 1, ngx))
     beside_y = (lax.rem(gy + ngy - 1, ngy), lax.rem(gy + 1, ngy))
@@ -126,8 +134,8 @@
         for s in (2 * r, 2 * r + 1):
             write(vel.at[s], everything, states[index_s[s]].astype(F32))
         for side in range(4):
-            parts = strips(vel.at[2 * r], side, (0, 1)) + strips(vel.at[2 * r + 1], side, (0,))
-            send_v[r, side] = pack(jnp.concatenate(parts, axis=0))
+            send_v[r, side] = pack(jnp.concatenate(strips(vel.at[2 * r], side, (0, 1)), axis=0))
+            send_w[r, side] = pack(jnp.concatenate(strips(vel.at[2 * r + 1], side, (0,)), axis=0))
 
     def stage_solved(r):
         for side in range(4):
@@ -158,6 +166,9 @@
     def speed_copy(r, side):
         return remote(send_v, recv_v, sv_sem, rv_sem, r, side, 1, beside)
 
+    def later_copy(r, side):
+        return remote(send_w, recv_w, sw_sem, rw_sem, r, side, 1, beside)
+
     def solved_copy(r, side):
         return remote(send_s, recv_s, ss_sem, rs_sem, r, side, 1, beside)
 
@@ -282,16 +293,16 @@
             stacked.astype(BF16), filters[...], (((1,), (1,)), ((), ())), preferred_element_type=F32
         )
 
-    loads[2].wait()
+    loads[halves].wait()
     whole = inverse[...]
     high = whole.astype(BF16)
     inv_hi[...] = high
     inv_lo[...] = (whole - high.astype(F32)).astype(BF16)
-    for load in loads[6:]:
+    for load in loads[:halves]:
         load.wait()
     write(solved, everything, product(read(adj, everything)))
-    loads[0].wait()
-    loads[1].wait()
+    loads[halves + 1].wait()
+    loads[halves + 2].wait()
     stage_speed(0)
     stage_solved(0)
 
@@ -300,8 +311,10 @@
         solved_copy(0, k).start()
         corner_copy(0, k).start()
         speed_copy(0, k).start()
-
-    for load in loads[3:6]:
+    for k in range(4):
+        later_copy(0, k).start()
+
+    for load in loads[halves + 3 :]:
         load.wait()
     wanted = jnp.zeros((2 * slots, cols), jnp.int32)
     for j in range(slots):
@@ -309,6 +322,17 @@
         wanted = jnp.where(rows == j, first, wanted)
         wanted = jnp.where(rows == slots + j, first + 1, wanted)
     pick[...] = jnp.where(wanted == places, 1.0, 0.0).astype(BF16)
+    slot_rows = lax.broadcasted_iota(jnp.int32, (slots, lanes), 0)
+    lane = lax.broadcasted_iota(jnp.int32, (slots, lanes), 1)
+    named = jnp.full((slots, lanes), turbines, jnp.int32)
+    for j in range(slots):
+        named = jnp.where(slot_rows == j, turbine_s[0, 0, j], named)
+    live[...] = jnp.where((named == lane) & (lane < turbines), 1.0, 0.0)
+    lane_row = lax.broadcasted_iota(jnp.int32, (1, lanes), 1)
+    owners = jnp.full((1, lanes), -1, jnp.int32)
+    for k in range(turbines):
+        owners = jnp.where(lane_row == k, owner_s[k], owners)
+    mine[...] = jnp.where(owners == me, 1.0, 0.0)
     history[...] = jnp.zeros_like(history)
     weight[...] = jnp.zeros_like(weight)
     terms[...] = jnp.zeros_like(terms)
@@ -321,6 +345,8 @@
             stage_speed(r + 1)
             for side in range(4):
                 speed_copy(r + 1, side).start()
+            for side in range(4):
+                later_copy(r + 1, side).start()
 
         local(first)
         sources = [history[i] for i in range(2)]
@@ -349,10 +375,11 @@
         local(second)
         start = 0
         for side in range(4):
+            later_copy(r, side ^ 1).wait_recv()
             width = sy if side < 2 else sx
             far = [split(outer[start + c * width : start + (c + 1) * width]) for c in range(comps)]
             start += comps * width
-            fix(second, side, far, triples(recv_v[r, side], side)[2])
+            fix(second, side, far, triples(recv_w[r, side], side)[0])
         history[1] = read(adj, pl.ds(0, cols)).astype(BF16)
 
         @pl.when(r < steps // 2 - 1)
@@ -377,43 +404,45 @@
     seen = look([history[i] for i in range(2)])
     total = terms[...] + weight[0] * seen[:slots] + weight[1] * seen[slots:]
     term = jnp.sum(total, axis=1, keepdims=True)
-    slot_rows = lax.broadcasted_iota(jnp.int32, (slots, lanes), 0)
-    lane = lax.broadcasted_iota(jnp.int32, (slots, lanes), 1)
-    named = jnp.full((slots, lanes), turbines, jnp.int32)
-    for j in range(slots):
-        named = jnp.where(slot_rows == j, turbine_s[0, 0, j], named)
-    live = (named == lane) & (lane < turbines)
-    part[...] = jnp.sum(jnp.where(live, term, 0.0), axis=0, keepdims=True)
+    part[...] = jnp.sum(live[...] * term, axis=0, keepdims=True)
 
     def share(k):
         return pltpu.make_async_remote_copy(
-            src_ref=part, dst_ref=got.at[k - 1],
-            send_sem=st_sem.at[k - 1], recv_sem=rt_sem.at[k - 1],
+            src_ref=part, dst_ref=got.at[k - 1], send_sem=st_sem, recv_sem=rt_sem,
             device_id=peer(k), device_id_type=MESH,
         )
 
-    def run(act):
-        def one(k, c):
-            act(share(k))
-            return c
-        lax.fori_loop(1, count, one, 0)
-
-    run(lambda c: c.start())
+    others(lambda k: share(k).start())
 
     def drain(r, c):
         for k in range(4):
             speed_copy(r, k).wait_send()
+            later_copy(r, k).wait_send()
             solved_copy(r, k).wait_send()
             corner_copy(r, k).wait_send()
         return c
 
     lax.fori_loop(0, steps // 2, drain, 0)
-    run(lambda c: c.wait_recv())
+    pltpu.make_async_copy(got, got, st_sem).wait()
+    pltpu.make_async_copy(got, got, rt_sem).wait()
     summed = part[...] + jnp.sum(got[...], axis=0)
-    total_ref[...] = summed[:, :turbines].reshape(total_ref.shape)
-    run(lambda c: c.wait_send())
+    grad[...] = jnp.where(mine[...] > 0.0, summed, 0.0)[:, :turbines].reshape(grad.shape)
+    last = pltpu.make_async_copy(grad, grad_hbm, out_sem.at[halves])
+    last.start()
+    last.wait()
     for out in outs:
         out.wait()
+
+
+def hand_over(parts, chunk, final_in, grad_in, final_out, grad_out, sem):
+    moves = [pltpu.make_async_copy(grad_in, grad_out, sem.at[parts])]
+    for k in range(parts):
+        rows = pl.ds(k * chunk, chunk)
+        moves.append(pltpu.make_async_copy(final_in.at[rows], final_out.at[rows], sem.at[k]))
+    for move in moves:
+        move.start()
+    for move in moves:
+        move.wait()
 
 
 def body(sizes, adjoint_init, saved_states, step_index, vertical_inverse, disk_filter,
@@ -435,14 +464,14 @@
     anywhere = pl.BlockSpec(memory_space=pl.ANY)
     halo = lambda rows: pltpu.VMEM((rounds, 4, rows, 128), BF16)
     dma = pltpu.SemaphoreType.DMA
-    final, totals = pl.pallas_call(
+    final, grad = pl.pallas_call(
         functools.partial(kernel, dims),
         out_shape=(
             jax.ShapeDtypeStruct((rows, levels), F32),
             jax.ShapeDtypeStruct((1, 1, turbines), F32),
         ),
-        in_specs=[pl.BlockSpec(memory_space=pltpu.HBM)] * 7,
-        out_specs=(anywhere, pl.BlockSpec(memory_space=pltpu.VMEM)),
+        in_specs=[pl.BlockSpec(memory_space=pltpu.HBM)] * 8,
+        out_specs=(anywhere, anywhere),
         scratch_shapes=[
             pltpu.VMEM((halves, rows, 128), F32),
             pltpu.VMEM((saved, rows, levels), BF16),
@@ -451,21 +480,25 @@
             pltpu.VMEM((slots * points, cells), BF16),
             pltpu.SMEM(pair_turbine.shape, jnp.int32),
             pltpu.SMEM(pair_tile.shape, jnp.int32),
+            pltpu.SMEM(turbine_owner.shape, jnp.int32),
             pltpu.VMEM((levels, levels), BF16),
             pltpu.VMEM((levels, levels), BF16),
             pltpu.VMEM((halves, rows, 128), F32),
             pltpu.VMEM((steps, halves, rows, 128), F32),
             pltpu.VMEM((2, sx * sy, levels), BF16),
             pltpu.VMEM((2 * slots, sx * sy), BF16),
+            pltpu.VMEM((slots, lanes), F32),
+            pltpu.VMEM((1, lanes), F32),
             pltpu.VMEM((2, slots, slots * points), F32),
             pltpu.VMEM((slots, slots * points), F32),
-            halo(3 * strip), halo(3 * strip), halo(2 * strip), halo(2 * strip),
+            pltpu.VMEM((1, 1, turbines), F32),
+            halo(2 * strip), halo(2 * strip), halo(strip), halo(strip), halo(2 * strip), halo(2 * strip),
             halo(8 * halves), halo(8 * halves),
             pltpu.VMEM((1, lanes), F32),
             pltpu.VMEM((count - 1, 1, lanes), F32),
-            dma((6 + halves,)), dma((halves,)),
-            *[dma((rounds, 4))] * 6,
-            dma((count - 1,)), dma((count - 1,)),
+            dma((7 + halves,)), dma((halves + 1,)),
+            *[dma((rounds, 4))] * 8,
+            dma, dma,
         ],
         compiler_params=pltpu.CompilerParams(
             collective_id=0, has_side_effects=True, vmem_limit_bytes=60 * 1024 * 1024
@@ -479,9 +512,21 @@
         disk_filter.reshape(slots * points, cells),
         pair_turbine,
         pair_tile,
+        turbine_owner,
     )
-    own = lax.axis_index("gx") * ngy + lax.axis_index("gy")
-    grad = jnp.where(turbine_owner[None, None, :] == own, totals, 0.0)
+    chunk = rows // comps
+    final, grad = pl.pallas_call(
+        functools.partial(hand_over, comps, chunk),
+        out_shape=(
+            jax.ShapeDtypeStruct((rows, levels), F32),
+            jax.ShapeDtypeStruct((1, 1, turbines), F32),
+        ),
+        in_specs=[anywhere] * 2,
+        out_specs=(anywhere, anywhere),
+        scratch_shapes=[dma((comps + 1,))],
+        compiler_params=pltpu.CompilerParams(vmem_limit_bytes=60 * 1024 * 1024),
+        name="hand_over",
+    )(final, grad)
     return final.reshape(adjoint_init.shape), grad
 
 

time: 27.6 us -> 31.2 us (1.13)
  Pallas kernels: 24 us -> 30.4 us
  local copies, waits for them, and re-layouts: 2.26 us -> 0 us
  other arithmetic: 0.51 us -> 0 us
    pallas_call x0 -> x1, Pallas kernels: none -> 7.11 us  [body(): pl.pallas_call(functools.partial(hand_over, comps, chunk), out_shape=(jax...]
    unnamed x5 -> x0, local copies, waits for them, and re-layouts: 2.26 us -> none
    pallas_call x1, Pallas kernels: 24 us -> 23.3 us  [body(): pl.pallas_call(functools.partial(kernel, dims), out_shape=(jax.ShapeDtype...]
    select_n x1 -> x0, other arithmetic: 0.51 us -> none  [body(): grad = jnp.where(turbine_owner[None, None, :] == own, totals, 0.0)]
where the time goes in v4:
time: 31.2 us; the launch traced here: 31.1 us
  Pallas kernels  30.4 us (97%)
  between operations  0.64 us (2%)
    pallas_call x1, Pallas kernels, body(): pl.pallas_call(functools.partial(kernel, dims), out_shape=(jax.ShapeDtype...  23.3 us
    pallas_call x1, Pallas kernels, body(): pl.pallas_call(functools.partial(hand_over, comps, chunk), out_shape=(jax...  7.11 us

profile of v4, /device:TPU:0, one launch (start us, length us, event | category | flops | bytes accessed | tf_op | source)
XLA Modules:
  0.0 31.1 jit_solution(11352695315821588234)
XLA Ops:
  0.6 23.3 %sweep.1 = (f32[192,256]{1,0:T(8,128)}, f32[1,1,24]{2,1,0:T(1,128)}) custom-call(f32[192,256]{1,0:T(8,128)} %bitcast.6, bf16[4,192,256]{2,1,0:T(8,128)(2,1)} %bitcast.5, s32[4]{0:T(128)} %index_hbm.1, f32[256,256]{1,0:T(8,128)} %inverse_hbm.1, bf16[512,512]{1,0:T(8,128)(2,1)} %bitcast.4, s32[1,1,8]{2,1,0:T(1,128)} %turbine_hbm.1, s32[1,1,8]{2,1,0:T(1,128)} %tile_hbm.1, ...), custom_call_target="tpu_custom_call" | custom-call | tf_op jit(solution)/shard_map/sweep/pallas_call | solution.py:467
  23.9 7.1 %hand_over.1 = (f32[192,256]{1,0:T(8,128)}, f32[1,1,24]{2,1,0:T(1,128)}) custom-call(f32[192,256]{1,0:T(8,128)} %get-tuple-element.6.final_in, f32[1,1,24]{2,1,0:T(1,128)} %get-tuple-element.7.grad_in), custom_call_target="tpu_custom_call" | custom-call | tf_op jit(solution)/shard_map/hand_over/pallas_call | solution.py:518

commit v5 on v4

--- a/solution.py
+++ b/solution.py
@@ -60,12 +60,12 @@
 def kernel(
     dims,
     init_hbm, states_hbm, index_hbm, inverse_hbm, filter_hbm, turbine_hbm, tile_hbm, owner_hbm,
-    out_hbm, grad_hbm,
+    out_ref, grad_ref,
     adj, states, index_s, inverse, filters, turbine_s, tile_s, owner_s,
-    inv_hi, inv_lo, solved, vel, history, pick, live, mine, weight, terms, grad,
+    inv_hi, inv_lo, solved, vel, history, pick, live, mine, weight, terms,
     send_v, recv_v, send_w, recv_w, send_s, recv_s, send_c, recv_c,
     part, got,
-    load_sem, out_sem, sv_sem, rv_sem, sw_sem, rw_sem, ss_sem, rs_sem, sc_sem, rc_sem, st_sem, rt_sem,
+    load_sem, sv_sem, rv_sem, sw_sem, rw_sem, ss_sem, rs_sem, sc_sem, rc_sem, st_sem, rt_sem,
 ):
     ngx, ngy, comps, sx, sy, steps, slots, points, turbines = dims
     cols = sx * sy
@@ -394,13 +394,6 @@
 
     lax.fori_loop(0, steps // 2, pair, 0)
 
-    outs = [
-        pltpu.make_async_copy(adj.at[k], out_hbm.at[:, pl.ds(128 * k, 128)], out_sem.at[k])
-        for k in range(halves)
-    ]
-    for out in outs:
-        out.start()
-
     seen = look([history[i] for i in range(2)])
     total = terms[...] + weight[0] * seen[:slots] + weight[1] * seen[slots:]
     term = jnp.sum(total, axis=1, keepdims=True)
@@ -413,6 +406,7 @@
         )
 
     others(lambda k: share(k).start())
+    out_ref[...] = read(adj, everything)
 
     def drain(r, c):
         for k in range(4):
@@ -426,12 +420,7 @@
     pltpu.make_async_copy(got, got, st_sem).wait()
     pltpu.make_async_copy(got, got, rt_sem).wait()
     summed = part[...] + jnp.sum(got[...], axis=0)
-    grad[...] = jnp.where(mine[...] > 0.0, summed, 0.0)[:, :turbines].reshape(grad.shape)
-    last = pltpu.make_async_copy(grad, grad_hbm, out_sem.at[halves])
-    last.start()
-    last.wait()
-    for out in outs:
-        out.wait()
+    grad_ref[...] = jnp.where(mine[...] > 0.0, summed, 0.0)[:, :turbines].reshape(grad_ref.shape)
 
 
 def hand_over(parts, chunk, final_in, grad_in, final_out, grad_out, sem):
@@ -467,11 +456,11 @@
     final, grad = pl.pallas_call(
         functools.partial(kernel, dims),
         out_shape=(
-            jax.ShapeDtypeStruct((rows, levels), F32),
-            jax.ShapeDtypeStruct((1, 1, turbines), F32),
+            pltpu.VMEM((rows, levels), F32),
+            pltpu.VMEM((1, 1, turbines), F32),
         ),
         in_specs=[pl.BlockSpec(memory_space=pltpu.HBM)] * 8,
-        out_specs=(anywhere, anywhere),
+        out_specs=(pl.BlockSpec(memory_space=pltpu.VMEM),) * 2,
         scratch_shapes=[
             pltpu.VMEM((halves, rows, 128), F32),
             pltpu.VMEM((saved, rows, levels), BF16),
@@ -491,12 +480,11 @@
             pltpu.VMEM((1, lanes), F32),
             pltpu.VMEM((2, slots, slots * points), F32),
             pltpu.VMEM((slots, slots * points), F32),
-            pltpu.VMEM((1, 1, turbines), F32),
             halo(2 * strip), halo(2 * strip), halo(strip), halo(strip), halo(2 * strip), halo(2 * strip),
             halo(8 * halves), halo(8 * halves),
             pltpu.VMEM((1, lanes), F32),
             pltpu.VMEM((count - 1, 1, lanes), F32),
-            dma((7 + halves,)), dma((halves + 1,)),
+            dma((7 + halves,)),
             *[dma((rounds, 4))] * 8,
             dma, dma,
         ],
@@ -524,7 +512,7 @@
         in_specs=[anywhere] * 2,
         out_specs=(anywhere, anywhere),
         scratch_shapes=[dma((comps + 1,))],
-        compiler_params=pltpu.CompilerParams(vmem_limit_bytes=60 * 1024 * 1024),
+        compiler_params=pltpu.CompilerParams(vmem_limit_bytes=1024 * 1024),
         name="hand_over",
     )(final, grad)
     return final.reshape(adjoint_init.shape), grad

time: 31.2 us -> 24.3 us (0.78)
  Pallas kernels: 30.4 us -> 23.5 us
    pallas_call x1, Pallas kernels: 7.11 us -> 0.71 us  [body(): pl.pallas_call(functools.partial(hand_over, comps, chunk), out_shape=(jax...]
    pallas_call x1, Pallas kernels: 23.3 us -> 22.8 us  [body(): pl.pallas_call(functools.partial(kernel, dims), out_shape=(pltpu.VMEM((ro...]
where the time goes in v5:
time: 24.3 us; the launch traced here: 24.1 us
  Pallas kernels  23.5 us (97%)
  between operations  0.64 us (3%)
    pallas_call x1, Pallas kernels, body(): pl.pallas_call(functools.partial(kernel, dims), out_shape=(pltpu.VMEM((ro...  22.8 us
    pallas_call x1, Pallas kernels, body(): pl.pallas_call(functools.partial(hand_over, comps, chunk), out_shape=(jax...  0.71 us

profile of v5, /device:TPU:0, one launch (start us, length us, event | category | flops | bytes accessed | tf_op | source)
XLA Modules:
  0.0 24.1 jit_solution(15742000691657152399)
XLA Ops:
  0.6 22.8 %sweep.1 = (f32[192,256]{1,0:T(8,128)S(1)}, f32[1,1,24]{2,1,0:T(1,128)S(1)}) custom-call(f32[192,256]{1,0:T(8,128)} %bitcast.6, bf16[4,192,256]{2,1,0:T(8,128)(2,1)} %bitcast.5, s32[4]{0:T(128)} %index_hbm.1, f32[256,256]{1,0:T(8,128)} %inverse_hbm.1, bf16[512,512]{1,0:T(8,128)(2,1)} %bitcast.4, s32[1,1,8]{2,1,0:T(1,128)} %turbine_hbm.1, ...), custom_call_target="tpu_custom_call" | custom-call | tf_op jit(solution)/shard_map/sweep/pallas_call | solution.py:456
  23.4 0.7 %hand_over.1 = (f32[192,256]{1,0:T(8,128)}, f32[1,1,24]{2,1,0:T(1,128)}) custom-call(f32[192,256]{1,0:T(8,128)S(1)} %get-tuple-element.6.final_in, f32[1,1,24]{2,1,0:T(1,128)S(1)} %get-tuple-element.7.grad_in), custom_call_target="tpu_custom_call" | custom-call | tf_op jit(solution)/shard_map/hand_over/pallas_call | solution.py:506

commit v6 on v5

--- a/solution.py
+++ b/solution.py
@@ -62,7 +62,7 @@
     init_hbm, states_hbm, index_hbm, inverse_hbm, filter_hbm, turbine_hbm, tile_hbm, owner_hbm,
     out_ref, grad_ref,
     adj, states, index_s, inverse, filters, turbine_s, tile_s, owner_s,
-    inv_hi, inv_lo, solved, vel, history, pick, live, mine, weight, terms,
+    inv_hi, inv_lo, solved, vel, slopes_at, history, pick, live, mine, weight, terms,
     send_v, recv_v, send_w, recv_w, send_s, recv_s, send_c, recv_c,
     part, got,
     load_sem, sv_sem, rv_sem, sw_sem, rw_sem, ss_sem, rs_sem, sc_sem, rc_sem, st_sem, rt_sem,
@@ -130,11 +130,14 @@
     def strips(view, side, depths):
         return [take(view, c, side, depth) for depth in depths for c in range(comps)]
 
-    def stage_speed(r):
-        for s in (2 * r, 2 * r + 1):
-            write(vel.at[s], everything, states[index_s[s]].astype(F32))
+    def stage_first(r):
+        write(vel.at[2 * r], everything, states[index_s[2 * r]].astype(F32))
         for side in range(4):
             send_v[r, side] = pack(jnp.concatenate(strips(vel.at[2 * r], side, (0, 1)), axis=0))
+
+    def stage_second(r):
+        write(vel.at[2 * r + 1], everything, states[index_s[2 * r + 1]].astype(F32))
+        for side in range(4):
             send_w[r, side] = pack(jnp.concatenate(strips(vel.at[2 * r + 1], side, (0,)), axis=0))
 
     def stage_solved(r):
@@ -185,26 +188,41 @@
         dot = functools.partial(jnp.dot, preferred_element_type=F32)
         return dot(hi, inv_hi[...]) + (dot(hi, inv_lo[...]) + dot(lo, inv_hi[...]))
 
-    def local(s):
-        def field(view, c, x):
-            if x < 0 or x >= sx:
-                return [jnp.zeros((sy, 128), F32)] * halves
-            return [view[k, pl.ds(c * cols + x * sy, sy), :] for k in range(halves)]
-
-        def diffs(view, c, x):
-            mid = field(view, c, x)
-            low, high = field(view, c, x - 1), field(view, c, x + 1)
-            return (
-                [high[k] - low[k] for k in range(halves)],
-                [row_diff(tile) for tile in mid],
-                depth_diff(mid),
-            )
-
+    def field(view, c, x):
+        if x < 0 or x >= sx:
+            return [jnp.zeros((sy, 128), F32)] * halves
+        return [view[k, pl.ds(c * cols + x * sy, sy), :] for k in range(halves)]
+
+    def diffs(view, c, x):
+        mid = field(view, c, x)
+        low, high = field(view, c, x - 1), field(view, c, x + 1)
+        return (
+            [high[k] - low[k] for k in range(halves)],
+            [row_diff(tile) for tile in mid],
+            depth_diff(mid),
+        )
+
+    def make_slopes(s):
+        for x in range(sx):
+            for c in range(comps):
+                made = diffs(vel.at[s], c, x)
+                for d in range(3):
+                    for k in range(halves):
+                        slopes_at[3 * c + d, k, pl.ds(x * sy, sy), :] = made[d][k]
+
+    def local(s, ready):
         speed = vel.at[s]
+
+        def speed_slopes(c, x):
+            if not ready:
+                return diffs(speed, c, x)
+            rows = pl.ds(x * sy, sy)
+            return [[slopes_at[3 * c + d, k, rows, :] for k in range(halves)] for d in range(3)]
+
         for x in range(sx):
             speeds = [field(speed, c, x) for c in range(comps)]
             now = [field(solved, c, x) for c in range(comps)]
-            slopes = [diffs(speed, c, x) for c in range(comps)]
+            slopes = [speed_slopes(c, x) for c in range(comps)]
             for c in range(comps):
                 own = diffs(solved, c, x)
                 for k in range(halves):
@@ -300,17 +318,18 @@
     inv_lo[...] = (whole - high.astype(F32)).astype(BF16)
     for load in loads[:halves]:
         load.wait()
-    write(solved, everything, product(read(adj, everything)))
     loads[halves + 1].wait()
     loads[halves + 2].wait()
-    stage_speed(0)
+    stage_first(0)
+    pl.semaphore_wait(barrier, count - 1)
+    for k in range(4):
+        speed_copy(0, k).start()
+    write(solved, everything, product(read(adj, everything)))
     stage_solved(0)
-
-    pl.semaphore_wait(barrier, count - 1)
     for k in range(4):
         solved_copy(0, k).start()
         corner_copy(0, k).start()
-        speed_copy(0, k).start()
+    stage_second(0)
     for k in range(4):
         later_copy(0, k).start()
 
@@ -342,13 +361,15 @@
 
         @pl.when(r < steps // 2 - 1)
         def _():
-            stage_speed(r + 1)
+            stage_first(r + 1)
+            stage_second(r + 1)
             for side in range(4):
                 speed_copy(r + 1, side).start()
             for side in range(4):
                 later_copy(r + 1, side).start()
 
-        local(first)
+        local(first, False)
+        make_slopes(second)
         sources = [history[i] for i in range(2)]
         sources += [read(vel.at[s], pl.ds(0, cols)).astype(BF16) for s in (first, second)]
         seen = look(sources)
@@ -372,7 +393,7 @@
         outer = product(jnp.concatenate(ring, axis=0))
         write(solved, everything, product(read(adj, everything)))
 
-        local(second)
+        local(second, True)
         start = 0
         for side in range(4):
             later_copy(r, side ^ 1).wait_recv()
@@ -474,6 +495,7 @@
             pltpu.VMEM((levels, levels), BF16),
             pltpu.VMEM((halves, rows, 128), F32),
             pltpu.VMEM((steps, halves, rows, 128), F32),
+            pltpu.VMEM((3 * comps, halves, sx * sy, 128), F32),
             pltpu.VMEM((2, sx * sy, levels), BF16),
             pltpu.VMEM((2 * slots, sx * sy), BF16),
             pltpu.VMEM((slots, lanes), F32),

time: 24.3 us -> 24.3 us (level)
  no operation moved by 1% of the time
where the time goes in v6:
time: 24.3 us; the launch traced here: 24.1 us
  Pallas kernels  23.5 us (97%)
  between operations  0.64 us (3%)
    pallas_call x1, Pallas kernels, body(): pl.pallas_call(functools.partial(kernel, dims), out_shape=(pltpu.VMEM((ro...  22.8 us
    pallas_call x1, Pallas kernels, body(): pl.pallas_call(functools.partial(hand_over, comps, chunk), out_shape=(jax...  0.71 us

profile of v6, /device:TPU:0, one launch (start us, length us, event | category | flops | bytes accessed | tf_op | source)
XLA Modules:
  0.0 24.1 jit_solution(13205521676830717844)
XLA Ops:
  0.6 22.8 %sweep.1 = (f32[192,256]{1,0:T(8,128)S(1)}, f32[1,1,24]{2,1,0:T(1,128)S(1)}) custom-call(f32[192,256]{1,0:T(8,128)} %bitcast.6, bf16[4,192,256]{2,1,0:T(8,128)(2,1)} %bitcast.5, s32[4]{0:T(128)} %index_hbm.1, f32[256,256]{1,0:T(8,128)} %inverse_hbm.1, bf16[512,512]{1,0:T(8,128)(2,1)} %bitcast.4, s32[1,1,8]{2,1,0:T(1,128)} %turbine_hbm.1, ...), custom_call_target="tpu_custom_call" | custom-call | tf_op jit(solution)/shard_map/sweep/pallas_call | solution.py:477
  23.4 0.7 %hand_over.1 = (f32[192,256]{1,0:T(8,128)}, f32[1,1,24]{2,1,0:T(1,128)}) custom-call(f32[192,256]{1,0:T(8,128)S(1)} %get-tuple-element.6.final_in, f32[1,1,24]{2,1,0:T(1,128)S(1)} %get-tuple-element.7.grad_in), custom_call_target="tpu_custom_call" | custom-call | tf_op jit(solution)/shard_map/hand_over/pallas_call | solution.py:528

commit v7 on v5

--- a/solution.py
+++ b/solution.py
@@ -137,9 +137,11 @@
             send_v[r, side] = pack(jnp.concatenate(strips(vel.at[2 * r], side, (0, 1)), axis=0))
             send_w[r, side] = pack(jnp.concatenate(strips(vel.at[2 * r + 1], side, (0,)), axis=0))
 
-    def stage_solved(r):
+    def stage_solved(r, go):
         for side in range(4):
             send_s[r, side] = pack(jnp.concatenate(strips(solved, side, (0, 1)), axis=0))
+            if go:
+                solved_copy(r, side).start()
         place = lax.broadcasted_iota(jnp.int32, (8, 128), 0)
         for q in range(4):
             cell = (q // 2) * (sx - 1) * sy + (q % 2) * (sy - 1)
@@ -304,7 +306,7 @@
     loads[halves + 1].wait()
     loads[halves + 2].wait()
     stage_speed(0)
-    stage_solved(0)
+    stage_solved(0, False)
 
     pl.semaphore_wait(barrier, count - 1)
     for k in range(4):
@@ -385,9 +387,8 @@
         @pl.when(r < steps // 2 - 1)
         def _():
             write(solved, everything, product(read(adj, everything)))
-            stage_solved(r + 1)
+            stage_solved(r + 1, True)
             for k in range(4):
-                solved_copy(r + 1, k).start()
                 corner_copy(r + 1, k).start()
 
         return carry

time: 24.3 us -> 24.2 us (level)
  no operation moved by 1% of the time
where the time goes in v7:
time: 24.2 us; the launch traced here: 24.1 us
  Pallas kernels  23.5 us (97%)
  between operations  0.64 us (3%)
    pallas_call x1, Pallas kernels, body(): pl.pallas_call(functools.partial(kernel, dims), out_shape=(pltpu.VMEM((ro...  22.7 us
    pallas_call x1, Pallas kernels, body(): pl.pallas_call(functools.partial(hand_over, comps, chunk), out_shape=(jax...  0.71 us

profile of v7, /device:TPU:0, one launch (start us, length us, event | category | flops | bytes accessed | tf_op | source)
XLA Modules:
  0.0 24.1 jit_solution(616614812177334591)
XLA Ops:
  0.6 22.7 %sweep.1 = (f32[192,256]{1,0:T(8,128)S(1)}, f32[1,1,24]{2,1,0:T(1,128)S(1)}) custom-call(f32[192,256]{1,0:T(8,128)} %bitcast.6, bf16[4,192,256]{2,1,0:T(8,128)(2,1)} %bitcast.5, s32[4]{0:T(128)} %index_hbm.1, f32[256,256]{1,0:T(8,128)} %inverse_hbm.1, bf16[512,512]{1,0:T(8,128)(2,1)} %bitcast.4, s32[1,1,8]{2,1,0:T(1,128)} %turbine_hbm.1, ...), custom_call_target="tpu_custom_call" | custom-call | tf_op jit(solution)/shard_map/sweep/pallas_call | solution.py:457
  23.4 0.7 %hand_over.1 = (f32[192,256]{1,0:T(8,128)}, f32[1,1,24]{2,1,0:T(1,128)}) custom-call(f32[192,256]{1,0:T(8,128)S(1)} %get-tuple-element.6.final_in, f32[1,1,24]{2,1,0:T(1,128)S(1)} %get-tuple-element.7.grad_in), custom_call_target="tpu_custom_call" | custom-call | tf_op jit(solution)/shard_map/hand_over/pallas_call | solution.py:507
